TPU v7x, 32 devices: a whole 2x2x4 slice. The times are simulated.
32 devices in a mesh: section: 2 (over core), rep: 4 (over z), fsdp: 4 (over y, x).
Axes of the slice: x: 2, y: 2, z: 4, core: 2. Of those that a mesh axis runs over, the one named last changes fastest.
Arguments:
- inputs: bfloat16 [2, 4, 1024, 576], P(None, 'rep', 'fsdp'), may hold values from -6 to 6
- cotangent: bfloat16 [2, 4, 1024, 576], P(None, 'rep', 'fsdp'), may hold values from -6 to 6
- segments: int32 [2, 4, 1024], P(None, 'rep'), may hold values from 0 to 17, as said below
- query_weight: bfloat16 [2, 576, 576], P('section', 'fsdp'), may hold values from -0.25 to 0.25
- key_weight: bfloat16 [2, 576, 192], P('section', 'fsdp'), may hold values from -0.25 to 0.25
- value_weight: bfloat16 [2, 576, 192], P('section', 'fsdp'), may hold values from -0.25 to 0.25
- output_weight: bfloat16 [2, 576, 576], P('section', 'fsdp'), may hold values from -1 to 1
- gate_weight: bfloat16 [2, 576, 1536], P('section', 'fsdp'), may hold values from -0.25 to 0.25
- up_weight: bfloat16 [2, 576, 1536], P('section', 'fsdp'), may hold values from -0.25 to 0.25
- down_weight: bfloat16 [2, 1536, 576], P('section', 'fsdp'), may hold values from -0.15625 to 0.15625
- attention_gain: bfloat16 [2, 576], P('section', 'fsdp'), may hold values from 0.25 to 1.75
- feedforward_gain: bfloat16 [2, 576], P('section', 'fsdp'), may hold values from 0.25 to 1.75
Outputs:
- section_output: bfloat16 [2, 2, 4, 1024, 576], P('section', None, 'rep', 'fsdp')
- input_grad: float32 [2, 2, 4, 1024, 576], P('section', None, 'rep', 'fsdp')
- query_grad: float32 [2, 576, 576], P('section', 'fsdp')
- key_grad: float32 [2, 576, 192], P('section', 'fsdp')
- value_grad: float32 [2, 576, 192], P('section', 'fsdp')
- output_grad: float32 [2, 576, 576], P('section', 'fsdp')
- gate_grad: float32 [2, 576, 1536], P('section', 'fsdp')
- up_grad: float32 [2, 576, 1536], P('section', 'fsdp')
- down_grad: float32 [2, 1536, 576], P('section', 'fsdp')
- attention_gain_grad: float32 [2, 576], P('section', 'fsdp')
- feedforward_gain_grad: float32 [2, 576], P('section', 'fsdp')
Inputs may be any that keep to these rules, and one draw needn't show every extreme that they name: `segments`: segment numbers of a sequence start at 0 and never fall; each document of a sequence with several documents holds 60 to 800 tokens, but the last of a sequence may be shorter; for each sequence index, the sequence of one micro-batch is a single document; in each draw one sequence of another micro-batch is cut into documents of exactly 60 tokens (its last may be shorter).
All inputs are finite; a program needn't handle non-finite values.
Results may differ from a plain program's by a relative error of at most 0.025.
Values may be sent and summed in bfloat16 or wider, within the bound.
A program may use at most 192 MiB of HBM per device.

v0:
```python
import jax
import jax.numpy as jnp
from jax import lax
from jax.sharding import PartitionSpec as P

QH = 9
KVH = 3
HD = 64


EPS_NORM = 1e-05
ROPE_BASE = 100000.0


def passed_along(block, axis, distance):
    devices = range(lax.axis_size(axis))
    route = [(i - distance, i) for i in devices if i - distance in devices]
    return lax.ppermute(block, axis, route)


def product(left, right):
    return jnp.dot(left, right, preferred_element_type=jnp.float32)


def product_tn(left, right):
    return lax.dot_general(
        left, right, (((0,), (0,)), ((), ())), preferred_element_type=jnp.float32
    )


def product_nt(left, right):
    return lax.dot_general(
        left, right, (((1,), (1,)), ((), ())), preferred_element_type=jnp.float32
    )


def norm_rows(values, gain):
    return values * lax.rsqrt(jnp.mean(values * values, -1, keepdims=True) + EPS_NORM) * gain


def doc_positions(segment_ids):
    places = jnp.arange(segment_ids.shape[0], dtype=jnp.int32)
    change = jnp.concatenate([jnp.ones((1,), jnp.bool_), segment_ids[1:] != segment_ids[:-1]])
    starts = jnp.where(change, places, jnp.zeros_like(places))
    firsts = lax.cummax(starts, axis=0)
    return (places - firsts).astype(jnp.float32)


def angle_table(positions, head_size):
    half = head_size // 2
    freqs = jnp.power(ROPE_BASE, -(jnp.arange(half, dtype=jnp.float32) * 2.0) / head_size)
    return positions[:, None] * freqs[None, :]


def rotary(tensor, angle):
    half = tensor.shape[-1] // 2
    cos_table = jnp.cos(angle)[:, None, :]
    sin_table = jnp.sin(angle)[:, None, :]
    front_half = tensor[..., :half]
    back_half = tensor[..., half:]
    return jnp.concatenate(
        [
            front_half * cos_table - back_half * sin_table,
            back_half * cos_table + front_half * sin_table,
        ],
        -1,
    )


def fetch_weights(shards):
    gathered = (
        lax.all_gather(shards[0], "fsdp", axis=1, tiled=True),
        lax.all_gather(shards[1], "fsdp", axis=1, tiled=True),
        lax.all_gather(shards[2], "fsdp", axis=1, tiled=True),
        lax.all_gather(shards[3], "fsdp", axis=1, tiled=True),
        lax.all_gather(shards[4], "fsdp", axis=1, tiled=True),
        lax.all_gather(shards[5], "fsdp", axis=1, tiled=True),
        lax.all_gather(shards[6], "fsdp", axis=1, tiled=True),
        lax.all_gather(shards[7], "fsdp", axis=1, tiled=True),
        lax.all_gather(shards[8], "fsdp", axis=1, tiled=True),
    )
    return tuple((piece[0] for piece in gathered))


def reduce_rows(parts):
    return (
        lax.psum_scatter(
            parts[0][None].astype(jnp.bfloat16), "fsdp", scatter_dimension=1, tiled=True
        ).astype(jnp.float32),
        lax.psum_scatter(
            parts[1][None].astype(jnp.bfloat16), "fsdp", scatter_dimension=1, tiled=True
        ).astype(jnp.float32),
        lax.psum_scatter(
            parts[2][None].astype(jnp.bfloat16), "fsdp", scatter_dimension=1, tiled=True
        ).astype(jnp.float32),
        lax.psum_scatter(
            parts[3][None].astype(jnp.bfloat16), "fsdp", scatter_dimension=1, tiled=True
        ).astype(jnp.float32),
        lax.psum_scatter(
            parts[4][None].astype(jnp.bfloat16), "fsdp", scatter_dimension=1, tiled=True
        ).astype(jnp.float32),
        lax.psum_scatter(
            parts[5][None].astype(jnp.bfloat16), "fsdp", scatter_dimension=1, tiled=True
        ).astype(jnp.float32),
        lax.psum_scatter(
            parts[6][None].astype(jnp.bfloat16), "fsdp", scatter_dimension=1, tiled=True
        ).astype(jnp.float32),
        lax.psum_scatter(
            parts[7][None].astype(jnp.bfloat16), "fsdp", scatter_dimension=1, tiled=True
        ).astype(jnp.float32),
        lax.psum_scatter(
            parts[8][None].astype(jnp.bfloat16), "fsdp", scatter_dimension=1, tiled=True
        ).astype(jnp.float32),
    )


def attend_forward(query_heads, key_heads, value_heads, allowed):
    group = query_heads.shape[0] // key_heads.shape[0]
    scale = query_heads.shape[-1] ** (-0.5)

    def one_head(item):
        query, head_index = item
        key = key_heads[head_index // group]
        value = value_heads[head_index // group]
        scores = product_nt(query, key) * scale
        scores = jnp.where(allowed, scores, -1e30)
        highest = jnp.max(scores, -1, keepdims=True)
        raised = jnp.exp(scores - highest)
        totals = jnp.sum(raised, -1, keepdims=True)
        weights = (raised / totals).astype(jnp.bfloat16)
        return (product(weights, value), (highest + jnp.log(totals))[:, 0])

    return lax.map(one_head, (query_heads, jnp.arange(query_heads.shape[0], dtype=jnp.int32)))


def attend_backward(query_heads, key_heads, value_heads, allowed, log_totals, grad_heads):
    heads_kv = key_heads.shape[0]
    group = query_heads.shape[0] // heads_kv
    scale = query_heads.shape[-1] ** (-0.5)

    def one_head(item):
        query, log_row, grad_out, head_index = item
        key = key_heads[head_index // group]
        value = value_heads[head_index // group]
        scores = product_nt(query, key) * scale
        scores = jnp.where(allowed, scores, -1e30)
        weights = jnp.exp(scores - log_row[:, None])
        grad_weights = product_nt(grad_out, value)
        grad_value = product_tn(weights.astype(jnp.bfloat16), grad_out)
        grad_scores = (
            weights * (grad_weights - jnp.sum(weights * grad_weights, -1, keepdims=True))
        ).astype(jnp.bfloat16)
        grad_query = product(grad_scores, key) * scale
        grad_key = product_tn(grad_scores, query) * scale
        return (grad_query, grad_key, grad_value)

    grad_query, grad_key, grad_value = lax.map(
        one_head,
        (query_heads, log_totals, grad_heads, jnp.arange(query_heads.shape[0], dtype=jnp.int32)),
    )
    length = key_heads.shape[1]
    grad_key = jnp.sum(grad_key.reshape(heads_kv, group, length, -1), axis=1)
    grad_value = jnp.sum(grad_value.reshape(heads_kv, group, length, -1), axis=1)
    return (grad_query, grad_key, grad_value)


def layer_forward(activation, weights, segment_ids, row_start):
    (
        query_weight,
        key_weight,
        value_weight,
        output_weight,
        gate_weight,
        up_weight,
        down_weight,
        attention_gain,
        feedforward_gain,
    ) = weights
    rows_here = activation.shape[0]
    length = segment_ids.shape[0]
    angle_all = angle_table(doc_positions(segment_ids), HD)
    angle = lax.dynamic_slice_in_dim(angle_all, row_start, rows_here, 0)
    normed = norm_rows(activation, attention_gain.astype(jnp.float32)).astype(jnp.bfloat16)
    queries = rotary(product(normed, query_weight).reshape(rows_here, QH, HD), angle).astype(
        jnp.bfloat16
    )
    keys_local = (
        rotary(product(normed, key_weight).reshape(rows_here, KVH, HD), angle)
        .astype(jnp.bfloat16)
        .reshape(rows_here, KVH * HD)
    )
    values_local = product(normed, value_weight).astype(jnp.bfloat16)
    keys_all, values_all = (
        lax.all_gather(keys_local, "fsdp", axis=0, tiled=True),
        lax.all_gather(values_local, "fsdp", axis=0, tiled=True),
    )
    places = jnp.arange(length, dtype=jnp.int32)
    own_places = row_start + jnp.arange(rows_here, dtype=jnp.int32)
    own_ids = lax.dynamic_slice_in_dim(segment_ids, row_start, rows_here, 0)
    allowed = (own_ids[:, None] == segment_ids[None, :]) & (own_places[:, None] >= places[None, :])
    query_heads = jnp.transpose(queries, (1, 0, 2))
    key_heads = jnp.transpose(keys_all.reshape(length, KVH, HD), (1, 0, 2))
    value_heads = jnp.transpose(values_all.reshape(length, KVH, HD), (1, 0, 2))
    heads_out, log_totals = attend_forward(query_heads, key_heads, value_heads, allowed)
    attended = jnp.transpose(heads_out, (1, 0, 2)).reshape(rows_here, QH * HD).astype(jnp.bfloat16)
    middle = activation + product(attended, output_weight)
    normed_mid = norm_rows(middle, feedforward_gain.astype(jnp.float32)).astype(jnp.bfloat16)
    gate_pre = product(normed_mid, gate_weight)
    lifted = product(normed_mid, up_weight)
    hidden = (jax.nn.silu(gate_pre) * lifted).astype(jnp.bfloat16)
    result = middle + product(hidden, down_weight)
    kept = (
        activation,
        normed,
        query_heads,
        key_heads,
        value_heads,
        allowed,
        log_totals,
        attended,
        middle,
        normed_mid,
        gate_pre,
        lifted,
        hidden,
        angle,
    )
    return (result, kept)


def layer_backward(grad_out, kept, weights):
    (
        query_weight,
        key_weight,
        value_weight,
        output_weight,
        gate_weight,
        up_weight,
        down_weight,
        attention_gain,
        feedforward_gain,
    ) = weights
    (
        activation,
        normed,
        query_heads,
        key_heads,
        value_heads,
        allowed,
        log_totals,
        attended,
        middle,
        normed_mid,
        gate_pre,
        lifted,
        hidden,
        angle,
    ) = kept
    rows_here = activation.shape[0]
    length = key_heads.shape[1]
    branch_grad = grad_out.astype(jnp.bfloat16)
    down_wgrad = product_tn(hidden, branch_grad)
    hidden_grad = product_nt(branch_grad, down_weight)
    sigma = jax.nn.sigmoid(gate_pre)
    gate_part = (hidden_grad * lifted * sigma * (1.0 + gate_pre * (1.0 - sigma))).astype(
        jnp.bfloat16
    )
    lift_part = (hidden_grad * gate_pre * sigma).astype(jnp.bfloat16)
    gate_wgrad = product_tn(normed_mid, gate_part)
    up_wgrad = product_tn(normed_mid, lift_part)
    normed_mid_grad = product_nt(gate_part, gate_weight) + product_nt(lift_part, up_weight)
    _, mid_pull = jax.vjp(norm_rows, middle, feedforward_gain.astype(jnp.float32))
    middle_part, ffn_gain_grad = mid_pull(normed_mid_grad)
    middle_grad = grad_out + middle_part
    attended_branch = middle_grad.astype(jnp.bfloat16)
    output_wgrad = product_tn(attended, attended_branch)
    attended_grad = product_nt(attended_branch, output_weight).astype(jnp.bfloat16)
    grad_heads = jnp.transpose(attended_grad.reshape(rows_here, QH, HD), (1, 0, 2))
    query_part, key_part, value_part = attend_backward(
        query_heads, key_heads, value_heads, allowed, log_totals, grad_heads
    )
    key_flat = jnp.transpose(key_part, (1, 0, 2)).reshape(length, KVH * HD)
    value_flat = jnp.transpose(value_part, (1, 0, 2)).reshape(length, KVH * HD)
    key_mine, value_mine = (
        lax.psum_scatter(
            key_flat.astype(jnp.bfloat16), "fsdp", scatter_dimension=0, tiled=True
        ).astype(jnp.float32),
        lax.psum_scatter(
            value_flat.astype(jnp.bfloat16), "fsdp", scatter_dimension=0, tiled=True
        ).astype(jnp.float32),
    )
    query_raw = (
        rotary(jnp.transpose(query_part, (1, 0, 2)), -angle)
        .reshape(rows_here, QH * HD)
        .astype(jnp.bfloat16)
    )
    key_raw = (
        rotary(key_mine.reshape(rows_here, KVH, HD), -angle)
        .reshape(rows_here, KVH * HD)
        .astype(jnp.bfloat16)
    )
    value_raw = value_mine.astype(jnp.bfloat16)
    query_wgrad = product_tn(normed, query_raw)
    key_wgrad = product_tn(normed, key_raw)
    value_wgrad = product_tn(normed, value_raw)
    normed_grad = (
        product_nt(query_raw, query_weight)
        + product_nt(key_raw, key_weight)
        + product_nt(value_raw, value_weight)
    )
    _, act_pull = jax.vjp(norm_rows, activation, attention_gain.astype(jnp.float32))
    act_part, attn_gain_grad = act_pull(normed_grad)
    return (
        middle_grad + act_part,
        (
            query_wgrad,
            key_wgrad,
            value_wgrad,
            output_wgrad,
            gate_wgrad,
            up_wgrad,
            down_wgrad,
            attn_gain_grad,
            ffn_gain_grad,
        ),
    )


def body(
    inputs,
    cotangent,
    segments,
    query_weight,
    key_weight,
    value_weight,
    output_weight,
    gate_weight,
    up_weight,
    down_weight,
    attention_gain,
    feedforward_gain,
):
    shards = (
        query_weight,
        key_weight,
        value_weight,
        output_weight,
        gate_weight,
        up_weight,
        down_weight,
        attention_gain,
        feedforward_gain,
    )
    section = lax.axis_index("section")
    on_first = section == 0
    batches = inputs.shape[0]
    rows_here = inputs.shape[2]
    width = inputs.shape[3]
    row_start = lax.axis_index("fsdp") * rows_here
    seg_all = segments[:, 0, :]
    incoming = jnp.zeros((rows_here, width), jnp.bfloat16)
    saved_ticks = []
    sent_ticks = []
    for tick in range(batches + 1):
        weights = fetch_weights(shards)
        batch_index = jnp.clip(tick - section, 0, batches - 1)
        segment_ids = lax.dynamic_index_in_dim(seg_all, batch_index, 0, keepdims=False)
        first_in = inputs[min(tick, batches - 1), 0].astype(jnp.float32)
        act_in = jnp.where(on_first, first_in, incoming.astype(jnp.float32))
        result, kept = layer_forward(act_in, weights, segment_ids, row_start)
        sent = result.astype(jnp.bfloat16)
        if tick < batches:
            incoming = passed_along(sent, "section", 1)
        saved_ticks.append(kept)
        sent_ticks.append(sent)
    section_output = jnp.stack(
        [jnp.where(on_first, sent_ticks[batch], sent_ticks[batch + 1]) for batch in range(batches)]
    )[None, :, None]
    returning = jnp.zeros((rows_here, width), jnp.bfloat16)
    grad_ticks = []
    owned = None
    for step in range(batches + 1):
        weights = fetch_weights(shards)
        batch_raw = batches - step - section
        valid = ((batch_raw >= 0) & (batch_raw < batches)).astype(jnp.float32)
        batch_index = jnp.clip(batch_raw, 0, batches - 1)
        upstream = lax.dynamic_index_in_dim(cotangent[:, 0], batch_index, 0, keepdims=False).astype(
            jnp.float32
        )
        grad_out = jnp.where(on_first, returning.astype(jnp.float32), upstream) * valid
        grad_in, weight_grads = layer_backward(grad_out, saved_ticks[batches - step], weights)
        handed_back = grad_in.astype(jnp.bfloat16)
        if step < batches:
            returning = passed_along(handed_back, "section", -1)
        grad_ticks.append(jnp.where(on_first, grad_in, handed_back.astype(jnp.float32)))
        reduced = reduce_rows(weight_grads)
        if owned is None:
            owned = reduced
        else:
            owned = tuple((left + right for left, right in zip(owned, reduced)))
    input_grad = jnp.stack(
        [
            jnp.where(on_first, grad_ticks[batches - batch], grad_ticks[batches - batch - 1])
            for batch in range(batches)
        ]
    )[None, :, None]
    summed = (
        lax.psum(owned[0].astype(jnp.bfloat16), "rep").astype(jnp.float32),
        lax.psum(owned[1].astype(jnp.bfloat16), "rep").astype(jnp.float32),
        lax.psum(owned[2].astype(jnp.bfloat16), "rep").astype(jnp.float32),
        lax.psum(owned[3].astype(jnp.bfloat16), "rep").astype(jnp.float32),
        lax.psum(owned[4].astype(jnp.bfloat16), "rep").astype(jnp.float32),
        lax.psum(owned[5].astype(jnp.bfloat16), "rep").astype(jnp.float32),
        lax.psum(owned[6].astype(jnp.bfloat16), "rep").astype(jnp.float32),
        lax.psum(owned[7].astype(jnp.bfloat16), "rep").astype(jnp.float32),
        lax.psum(owned[8].astype(jnp.bfloat16), "rep").astype(jnp.float32),
    )
    return (
        section_output,
        input_grad,
        summed[0],
        summed[1],
        summed[2],
        summed[3],
        summed[4],
        summed[5],
        summed[6],
        summed[7],
        summed[8],
    )


def solution(mesh):
    placed = (
        P(None, "rep", "fsdp", None),
        P(None, "rep", "fsdp", None),
        P(None, "rep", None),
        P("section", "fsdp", None),
        P("section", "fsdp", None),
        P("section", "fsdp", None),
        P("section", "fsdp", None),
        P("section", "fsdp", None),
        P("section", "fsdp", None),
        P("section", "fsdp", None),
        P("section", "fsdp"),
        P("section", "fsdp"),
    )
    return jax.shard_map(
        body,
        mesh=mesh,
        in_specs=placed,
        out_specs=(
            P("section", None, "rep", "fsdp", None),
            P("section", None, "rep", "fsdp", None),
            P("section", "fsdp", None),
            P("section", "fsdp", None),
            P("section", "fsdp", None),
            P("section", "fsdp", None),
            P("section", "fsdp", None),
            P("section", "fsdp", None),
            P("section", "fsdp", None),
            P("section", "fsdp"),
            P("section", "fsdp"),
        ),
        check_vma=False,
    )
```

profile of v0, /device:TPU:0, one launch (start us, length us, event | category | flops | bytes accessed | tf_op | source)
XLA Modules:
  0.0 1715.2 jit_solution(9027276019583319541)
XLA Ops:
  10.2 13.4 all_gather.31
  91.6 50.6 %while.96 = (s32[]{:T(128)}, bf16[9,256,64]{1,2,0:T(8,128)(2,1)S(1)}, f32[9,256]{1,0:T(8,128)S(1)}, bf16[9,256,64]{2,1,0:T(8,128)(2,1)}, s32[9]{0:T(128)S(1)}, /...) while((s32[]{:T(128)}, ...), condition=%wide.region_6.7_spmd.clone, body=%wide.region_3.6_spmd.clone.sunk | while | flops 69992208 | bytes 3817781 | solution.py:133
  196.2 56.9 %while.97 = (s32[]{:T(128)}, bf16[9,256,64]{1,2,0:T(8,128)(2,1)}, f32[9,256]{1,0:T(8,128)S(1)}, bf16[9,256,64]{2,1,0:T(8,128)(2,1)}, s32[9]{0:T(128)S(1)}, /*ind...) while((s32[]{:T(128)}, bf16[9,256,64]{1,2,0:T(8,128)(2,1)}, ...), condition=%wide.region_14.15_spmd.clone, body=%wide.region_11.14_spmd.clone.sunk | while | flops 69992208 | bytes 3817781 | solution.py:133
  298.8 74.0 %while.98 = (s32[]{:T(128)}, bf16[9,256,64]{1,2,0:T(8,128)(2,1)}, f32[9,256]{1,0:T(8,128)}, bf16[9,256,64]{2,1,0:T(8,128)(2,1)}, s32[9]{0:T(128)}, /*index=5*/bf...) while((s32[]{:T(128)}, bf16[9,256,64]{1,2,0:T(8,128)(2,1)}, ...), condition=%wide.region_22.23_spmd.clone, body=%wide.region_19.22_spmd.clone.sunk | while | flops 69992208 | bytes 3817781 | solution.py:133
  389.4 106.3 %while.99 = (s32[]{:T(128)}, f32[9,256,64]{1,2,0:T(8,128)}, f32[9,1024,64]{1,2,0:T(8,128)}, f32[9,1024,64]{1,2,0:T(8,128)}, bf16[9,256,64]{2,1,0:T(8,128)(2,1)},...) while((s32[]{:T(128)}, f32[9,256,64]{1,2,0:T(8,128)}, ...), condition=%wide.region_27.28_spmd.clone, body=%wide.region_25.27_spmd.clone.sunk | while | flops 170999568 | bytes 9516373 | solution.py:157
  503.1 19.9 %reduce-scatter.70.cloned.1.call-done = bf16[256,192]{0,1:T(8,128)(2,1)} async-done(((bf16[1024,192]{0,1:T(8,128)(2,1)}), bf16[256,192]{0,1:T(8,128)(2,1)}) %reduce-scatter.70.cloned.1.call-update) | async-done | bytes 98320 | tf_op jit(solution)/shard_map/reduce_scatter | solution.py:285
  528.0 22.2 %reduce-scatter.72.cloned.1.call-done = bf16[256,192]{0,1:T(8,128)(2,1)} async-done(((bf16[1024,192]{0,1:T(8,128)(2,1)}), bf16[256,192]{0,1:T(8,128)(2,1)}) %reduce-scatter.72.cloned.1.call-update) | async-done | bytes 98320 | tf_op jit(solution)/shard_map/reduce_scatter | solution.py:288
  580.5 114.0 %while.100 = (s32[]{:T(128)}, f32[9,256,64]{1,2,0:T(8,128)}, f32[9,1024,64]{1,2,0:T(8,128)}, f32[9,1024,64]{1,2,0:T(8,128)}, bf16[9,256,64]{2,1,0:T(8,128)(2,1)}...) while((s32[]{:T(128)}, f32[9,256,64]{1,2,0:T(8,128)}, ...), condition=%wide.region_36.37_spmd.clone, body=%wide.region_34.36_spmd.clone.sunk | while | flops 170999568 | bytes 9516373 | solution.py:157
  702.0 21.1 %reduce-scatter.74.cloned.1.call-done = bf16[256,192]{0,1:T(8,128)(2,1)} async-done(((bf16[1024,192]{0,1:T(8,128)(2,1)}), bf16[256,192]{0,1:T(8,128)(2,1)}) %reduce-scatter.74.cloned.1.call-update) | async-done | bytes 98320 | tf_op jit(solution)/shard_map/reduce_scatter | solution.py:285
  728.0 22.9 %reduce-scatter.76.cloned.1.call-done = bf16[256,192]{0,1:T(8,128)(2,1)} async-done(((bf16[1024,192]{0,1:T(8,128)(2,1)}), bf16[256,192]{0,1:T(8,128)(2,1)}) %reduce-scatter.76.cloned.1.call-update) | async-done | bytes 98320 | tf_op jit(solution)/shard_map/reduce_scatter | solution.py:288
  771.0 100.2 %while.101 = (s32[]{:T(128)}, f32[9,256,64]{1,2,0:T(8,128)}, f32[9,1024,64]{1,2,0:T(8,128)S(1)}, f32[9,1024,64]{1,2,0:T(8,128)}, bf16[9,256,64]{2,1,0:T(8,128)(2...) while((s32[]{:T(128)}, f32[9,256,64]{1,2,0:T(8,128)}, ...), condition=%wide.region_45.46_spmd.clone, body=%wide.region_43.45_spmd.clone.sunk | while | flops 170999568 | bytes 9516717 | solution.py:157
  900.6 24.1 %reduce-scatter.80.cloned.1.call-done = bf16[256,192]{0,1:T(8,128)(2,1)} async-done(((bf16[1024,192]{0,1:T(8,128)(2,1)}), bf16[256,192]{0,1:T(8,128)(2,1)}) %reduce-scatter.80.cloned.1.call-update) | async-done | bytes 98320 | tf_op jit(solution)/shard_map/reduce_scatter | solution.py:288
  1006.5 25.9 %reduce-scatter.102.cloned.1.call-done = bf16[144,192]{1,0:T(8,128)(2,1)} async-done(((bf16[576,192]{1,0:T(8,128)(2,1)}), bf16[144,192]{1,0:T(8,128)(2,1)}) %reduce-scatter.102.cloned.1.call-update) | async-done | bytes 55312
  1036.1 15.1 all-reduce.14
  1060.3 25.8 %reduce-scatter.104.cloned.1.call-done = bf16[144,192]{1,0:T(8,128)(2,1)} async-done(((bf16[576,192]{1,0:T(8,128)(2,1)}), bf16[144,192]{1,0:T(8,128)(2,1)}) %reduce-scatter.104.cloned.1.call-update) | async-done | bytes 55312
  1088.6 26.1 %reduce-scatter.112.cloned.1.call-done = bf16[1,144,576]{2,1,0:T(8,128)(2,1)} async-done(((bf16[1,576,576]{2,1,0:T(8,128)(2,1)}), bf16[1,144,576]{2,1,0:T(8,128)(2,1)}) %reduce-scatter.112.cloned.1.call-update) | async-done | bytes 165904
  1114.7 28.6 %reduce-scatter.114.cloned.1.call-done = bf16[1,144,576]{2,1,0:T(8,128)(2,1)} async-done(((bf16[1,576,576]{2,1,0:T(8,128)(2,1)}), bf16[1,144,576]{2,1,0:T(8,128)(2,1)}) %reduce-scatter.114.cloned.1.call-update) | async-done | bytes 165904
  1143.3 29.2 %reduce-scatter.116.cloned.1.call-done = bf16[1,144,576]{2,1,0:T(8,128)(2,1)} async-done(((bf16[1,576,576]{2,1,0:T(8,128)(2,1)}), bf16[1,144,576]{2,1,0:T(8,128)(2,1)}) %reduce-scatter.116.cloned.1.call-update) | async-done | bytes 165904
  1174.3 26.9 %reduce-scatter.118.cloned.1.call-done = bf16[1,144,576]{2,1,0:T(8,128)(2,1)} async-done(((bf16[1,576,576]{2,1,0:T(8,128)(2,1)}), bf16[1,144,576]{2,1,0:T(8,128)(2,1)}) %reduce-scatter.118.cloned.1.call-update) | async-done | bytes 165904
  1201.2 28.6 %reduce-scatter.120.cloned.1.call-done = bf16[1,144,576]{2,1,0:T(8,128)(2,1)} async-done(((bf16[1,576,576]{2,1,0:T(8,128)(2,1)}), bf16[1,144,576]{2,1,0:T(8,128)(2,1)}) %reduce-scatter.120.cloned.1.call-update) | async-done | bytes 165904
  1229.9 28.8 %reduce-scatter.122.cloned.1.call-done = bf16[1,144,576]{2,1,0:T(8,128)(2,1)} async-done(((bf16[1,576,576]{2,1,0:T(8,128)(2,1)}), bf16[1,144,576]{2,1,0:T(8,128)(2,1)}) %reduce-scatter.122.cloned.1.call-update) | async-done | bytes 165904
  1260.5 35.4 %reduce-scatter.106.cloned.1.call-done = bf16[384,576]{1,0:T(8,128)(2,1)} async-done(((bf16[1536,576]{1,0:T(8,128)(2,1)}), bf16[384,576]{1,0:T(8,128)(2,1)}) %reduce-scatter.106.cloned.1.call-update) | async-done | bytes 442384
  1299.1 33.9 %reduce-scatter.108.cloned.1.call-done = bf16[384,576]{1,0:T(8,128)(2,1)} async-done(((bf16[1536,576]{1,0:T(8,128)(2,1)}), bf16[384,576]{1,0:T(8,128)(2,1)}) %reduce-scatter.108.cloned.1.call-update) | async-done | bytes 442384
  1336.3 33.8 %reduce-scatter.110.cloned.1.call-done = bf16[384,576]{1,0:T(8,128)(2,1)} async-done(((bf16[1536,576]{1,0:T(8,128)(2,1)}), bf16[384,576]{1,0:T(8,128)(2,1)}) %reduce-scatter.110.cloned.1.call-update) | async-done | bytes 442384
  1373.3 32.3 %reduce-scatter.82.cloned.1.call-done = bf16[1,144,1536]{2,1,0:T(8,128)(2,1)} async-done(((bf16[1,576,1536]{2,1,0:T(8,128)(2,1)}), bf16[1,144,1536]{2,1,0:T(8,128)(2,1)}) %reduce-scatter.82.cloned.1.call-update) | async-done | bytes 442384 | tf_op jit(solution)/shard_map/reduce_scatter | solution.py:99
  1405.6 35.4 %reduce-scatter.84.cloned.1.call-done = bf16[1,144,1536]{2,1,0:T(8,128)(2,1)} async-done(((bf16[1,576,1536]{2,1,0:T(8,128)(2,1)}), bf16[1,144,1536]{2,1,0:T(8,128)(2,1)}) %reduce-scatter.84.cloned.1.call-update) | async-done | bytes 442384 | tf_op jit(solution)/shard_map/reduce_scatter | solution.py:99
  1441.0 35.4 %reduce-scatter.86.cloned.1.call-done = bf16[1,144,1536]{2,1,0:T(8,128)(2,1)} async-done(((bf16[1,576,1536]{2,1,0:T(8,128)(2,1)}), bf16[1,144,1536]{2,1,0:T(8,128)(2,1)}) %reduce-scatter.86.cloned.1.call-update) | async-done | bytes 442384 | tf_op jit(solution)/shard_map/reduce_scatter | solution.py:99
  1478.6 33.3 %reduce-scatter.88.cloned.1.call-done = bf16[1,144,1536]{2,1,0:T(8,128)(2,1)} async-done(((bf16[1,576,1536]{2,1,0:T(8,128)(2,1)}), bf16[1,144,1536]{2,1,0:T(8,128)(2,1)}) %reduce-scatter.88.cloned.1.call-update) | async-done | bytes 442384 | tf_op jit(solution)/shard_map/reduce_scatter | solution.py:102
  1511.9 35.5 %reduce-scatter.90.cloned.1.call-done = bf16[1,144,1536]{2,1,0:T(8,128)(2,1)} async-done(((bf16[1,576,1536]{2,1,0:T(8,128)(2,1)}), bf16[1,144,1536]{2,1,0:T(8,128)(2,1)}) %reduce-scatter.90.cloned.1.call-update) | async-done | bytes 442384 | tf_op jit(solution)/shard_map/reduce_scatter | solution.py:102
  1547.5 35.4 %reduce-scatter.92.cloned.1.call-done = bf16[1,144,1536]{2,1,0:T(8,128)(2,1)} async-done(((bf16[1,576,1536]{2,1,0:T(8,128)(2,1)}), bf16[1,144,1536]{2,1,0:T(8,128)(2,1)}) %reduce-scatter.92.cloned.1.call-update) | async-done | bytes 442384 | tf_op jit(solution)/shard_map/reduce_scatter | solution.py:102
  1593.7 28.0 %all-reduce.21.cloned.1.call-done = (bf16[1,144,192]{1,2,0:T(8,128)(2,1)}, bf16[1,144,192]{1,2,0:T(8,128)(2,1)}, bf16[1,144]{1,0:T(2,128)(2,1)}, bf16[1,144]{1,0:T(2,128)(2,1)}) async-done(((bf16[1,144,192]{1,2,0:T(8,128)(2,1)}, bf16[1,144,192]{1,2,0:T(8,128)(2,1)}, bf16[1,144]{1,0:T(2,128)(2,1)}, bf16[1,144]{1,0:T(2,128)(2,1)}), (bf16[1,144,192]{1,2,0:T(8,128)(2,1)}, bf16[1,144,192]{1,2,0:T(8,128)(2,1)}, ...) | async-done | bytes 111184 | tf_op jit(solution)/shard_map/psum | solution.py:409
  1627.5 73.4 %all-reduce.23.cloned.1.call-done = (bf16[1,144,576]{2,1,0:T(8,128)(2,1)}, bf16[1,144,576]{2,1,0:T(8,128)(2,1)}, bf16[1,144,1536]{2,1,0:T(8,128)(2,1)}, bf16[1,144,1536]{2,1,0:T(8,128)(2,1)}, bf16[1,384,576]{1,2,0:T(8,128)(2,1)}) async-done(((bf16[1,144,576]{2,1,0:T(8,128)(2,1)}, bf16[1,144,576]{2,1,0:T(8,128)(2,1)}, bf16[1,144,1536]{2,1,0:T(8,128)(2,1)}, bf16[1,144,1536]{2,1,0:T(8,128)(2,1)}, ...) | async-done | bytes 1658896 | tf_op jit(solution)/shard_map/psum | solution.py:408
  (1041 shorter events, 819.0 us)
Async XLA Ops:
  7.2 147.6 %all-gather.4.cloned.1.call-start = ((), (), s32[]{:S(2)}) async-start(), calls=%async_computation.27 | async-start | bytes 2211840 | tf_op jit(solution)/shard_map/all_gather | solution.py:76
  7.9 150.4 %all-gather.6.cloned.1.call-start = ((), (), s32[]{:S(2)}) async-start(), calls=%async_computation.28 | async-start | bytes 2211840 | tf_op jit(solution)/shard_map/all_gather | solution.py:77
  8.7 153.9 %all-gather.8.cloned.1.call-start = ((), (), s32[]{:S(2)}) async-start(), calls=%async_computation.29 | async-start | bytes 2211840 | tf_op jit(solution)/shard_map/all_gather | solution.py:78
  9.5 513.6 %reduce-scatter.70.cloned.1.call-start = ((), (), s32[]{:S(2)}) async-start(), calls=%async_computation.30 | async-start | bytes 491520 | tf_op jit(solution)/shard_map/reduce_scatter | solution.py:285
  498.4 51.8 %reduce-scatter.72.cloned.1.call-start = ((), (), s32[]{:S(2)}) async-start(), calls=%async_computation.31 | async-start | bytes 491520 | tf_op jit(solution)/shard_map/reduce_scatter | solution.py:288
  503.1 220.0 %reduce-scatter.74.cloned.1.call-start = ((), (), s32[]{:S(2)}) async-start(), calls=%async_computation.32 | async-start | bytes 491520 | tf_op jit(solution)/shard_map/reduce_scatter | solution.py:285
  697.3 53.6 %reduce-scatter.76.cloned.1.call-start = ((), (), s32[]{:S(2)}) async-start(), calls=%async_computation.33 | async-start | bytes 491520 | tf_op jit(solution)/shard_map/reduce_scatter | solution.py:288
  702.0 194.9 %reduce-scatter.78.cloned.1.call-start = ((), (), s32[]{:S(2)}) async-start(), calls=%async_computation.34 | async-start | bytes 491520 | tf_op jit(solution)/shard_map/reduce_scatter | solution.py:285
  872.3 52.4 %reduce-scatter.80.cloned.1.call-start = ((), (), s32[]{:S(2)}) async-start(), calls=%async_computation.35 | async-start | bytes 491520 | tf_op jit(solution)/shard_map/reduce_scatter | solution.py:288
  875.1 116.8 %reduce-scatter.94.cloned.1.call-start = ((), (), s32[]{:S(2)}) async-start(), calls=%async_computation.42 | async-start | bytes 368640
  877.4 115.6 %reduce-scatter.100.cloned.1.call-start = ((), (), s32[]{:S(2)}) async-start(), calls=%async_computation.45 | async-start | bytes 368640
  879.5 125.9 %reduce-scatter.96.cloned.1.call-start = ((), (), s32[]{:S(2)}) async-start(), calls=%async_computation.43 | async-start | bytes 368640
  881.6 150.8 %reduce-scatter.102.cloned.1.call-start = ((), (), s32[]{:S(2)}) async-start(), calls=%async_computation.46 | async-start | bytes 368640
  883.7 175.6 %reduce-scatter.98.cloned.1.call-start = ((), (), s32[]{:S(2)}) async-start(), calls=%async_computation.44 | async-start | bytes 368640
  900.5 185.5 %reduce-scatter.104.cloned.1.call-start = ((), (), s32[]{:S(2)}) async-start(), calls=%async_computation.47 | async-start | bytes 368640
  927.6 187.1 %reduce-scatter.112.cloned.1.call-start = ((), (), s32[]{:S(2)}) async-start(), calls=%async_computation.51 | async-start | bytes 921600
  929.0 214.3 %reduce-scatter.114.cloned.1.call-start = ((), (), s32[]{:S(2)}) async-start(), calls=%async_computation.52 | async-start | bytes 921600
  930.4 242.1 %reduce-scatter.116.cloned.1.call-start = ((), (), s32[]{:S(2)}) async-start(), calls=%async_computation.53 | async-start | bytes 921600
  933.1 268.1 %reduce-scatter.118.cloned.1.call-start = ((), (), s32[]{:S(2)}) async-start(), calls=%async_computation.54 | async-start | bytes 921600
  934.5 295.3 %reduce-scatter.120.cloned.1.call-start = ((), (), s32[]{:S(2)}) async-start(), calls=%async_computation.55 | async-start | bytes 921600
  936.9 321.7 %reduce-scatter.122.cloned.1.call-start = ((), (), s32[]{:S(2)}) async-start(), calls=%async_computation.56 | async-start | bytes 921600
  938.3 357.6 %reduce-scatter.106.cloned.1.call-start = ((), (), s32[]{:S(2)}) async-start(), calls=%async_computation.48 | async-start | bytes 2457600
  949.9 383.1 %reduce-scatter.108.cloned.1.call-start = ((), (), s32[]{:S(2)}) async-start(), calls=%async_computation.49 | async-start | bytes 2457600
  961.6 408.5 %reduce-scatter.110.cloned.1.call-start = ((), (), s32[]{:S(2)}) async-start(), calls=%async_computation.50 | async-start | bytes 2457600
  973.3 432.3 %reduce-scatter.82.cloned.1.call-start = ((), (), s32[]{:S(2)}) async-start(), calls=%async_computation.36 | async-start | bytes 2211840 | tf_op jit(solution)/shard_map/reduce_scatter | solution.py:99
  976.5 464.6 %reduce-scatter.84.cloned.1.call-start = ((), (), s32[]{:S(2)}) async-start(), calls=%async_computation.37 | async-start | bytes 2211840 | tf_op jit(solution)/shard_map/reduce_scatter | solution.py:99
  979.5 496.9 %reduce-scatter.86.cloned.1.call-start = ((), (), s32[]{:S(2)}) async-start(), calls=%async_computation.38 | async-start | bytes 2211840 | tf_op jit(solution)/shard_map/reduce_scatter | solution.py:99
  982.7 529.2 %reduce-scatter.88.cloned.1.call-start = ((), (), s32[]{:S(2)}) async-start(), calls=%async_computation.39 | async-start | bytes 2211840 | tf_op jit(solution)/shard_map/reduce_scatter | solution.py:102
  984.9 562.6 %reduce-scatter.90.cloned.1.call-start = ((), (), s32[]{:S(2)}) async-start(), calls=%async_computation.40 | async-start | bytes 2211840 | tf_op jit(solution)/shard_map/reduce_scatter | solution.py:102
  987.9 595.0 %reduce-scatter.92.cloned.1.call-start = ((), (), s32[]{:S(2)}) async-start(), calls=%async_computation.41 | async-start | bytes 2211840 | tf_op jit(solution)/shard_map/reduce_scatter | solution.py:102
  991.0 630.7 %all-reduce.21.cloned.1.call-start = ((), (), s32[]{:S(2)}) async-start(), calls=%async_computation.57 | async-start | bytes 397312 | tf_op jit(solution)/shard_map/psum | solution.py:409
  1088.6 612.3 %all-reduce.23.cloned.1.call-start = ((), (), s32[]{:S(2)}) async-start(), calls=%async_computation.58 | async-start | bytes 3391488 | tf_op jit(solution)/shard_map/psum | solution.py:408
  (163 other events, 1561.4 us)
Sparse Core Ops, SparseCore 0:
  9.9 36.1 all-gather.3
  47.9 37.0 all-gather.5
  86.8 32.5 all-gather.7
  498.5 24.5 reduce-scatter.69
  525.7 24.4 reduce-scatter.71
  697.4 25.6 reduce-scatter.73
  726.5 24.3 reduce-scatter.75
  872.4 24.4 reduce-scatter.77
  900.2 24.4 reduce-scatter.79
  927.3 24.1 reduce-scatter.93
  954.3 24.1 reduce-scatter.99
  981.1 24.2 reduce-scatter.95
  1008.2 24.1 reduce-scatter.101
  1035.0 24.1 reduce-scatter.97
  1061.9 24.1 reduce-scatter.103
  1088.9 25.7 reduce-scatter.111
  1117.5 25.7 reduce-scatter.113
  1146.7 25.7 reduce-scatter.115
  1175.4 25.7 reduce-scatter.117
  1204.0 25.7 reduce-scatter.119
  1232.8 25.7 reduce-scatter.121
  1261.7 34.0 reduce-scatter.105
  1298.9 34.0 reduce-scatter.107
  1336.0 34.0 reduce-scatter.109
  1373.1 32.4 reduce-scatter.81
  1408.5 32.4 reduce-scatter.83
  1443.9 32.4 reduce-scatter.85
  1479.4 32.4 reduce-scatter.87
  1515.0 32.4 reduce-scatter.89
  1550.3 32.4 reduce-scatter.91
  1586.6 35.0 all-reduce.20
  1625.8 74.9 all-reduce.22
where the time goes:
time: 1740 us; the launch traced here: 1720 us
  waiting for transfers between devices  778 us (45%)
  matrix products  394 us (23%)
  local copies, waits for them, and re-layouts  184 us (11%)
  blocking collectives  140 us (8%)
  loops' own time  108 us (6%)
  other arithmetic  77.1 us (4%)
  between operations  18.3 us (1%)
    unnamed x47, waiting for transfers between devices  343 us
    dot_general x102, matrix products, product_nt(): lax.dot_general(left, right, (((1,), (1,)), ((), ())), preferred_element_...  146 us
    dot_general x75, matrix products, product(): return jnp.dot(left, right, preferred_element_type=jnp.float32)  126 us
    dot_general x75, matrix products, product_tn(): lax.dot_general(left, right, (((0,), (0,)), ((), ())), preferred_element_...  122 us
    reduce_scatter x3, waiting for transfers between devices, reduce_rows(): lax.psum_scatter(parts[5][None].astype(jnp.bfloat16), 'fsdp', scatter_dim...  104 us
    reduce_scatter x3, waiting for transfers between devices, reduce_rows(): lax.psum_scatter(parts[4][None].astype(jnp.bfloat16), 'fsdp', scatter_dim...  103 us
    unnamed x333, local copies, waits for them, and re-layouts  82.7 us
    psum x1, waiting for transfers between devices, body(): lax.psum(owned[0].astype(jnp.bfloat16), 'rep').astype(jnp.float32)  73.4 us
  transfers between devices with their start and end apart: 36, of which 28 were waited for; matrix products, arithmetic and copies ran while one was open for 11% of the time, Pallas kernels for 0%

commit v1 on v0

v1 whole, which is shorter than its diff:
```python
import functools

import jax
import jax.numpy as jnp
from jax import lax
from jax.experimental import pallas as pl
from jax.experimental.pallas import tpu as pltpu
from jax.sharding import PartitionSpec as P

QH = 9
KVH = 3
HD = 64
QD = QH * HD
KD = KVH * HD
GROUP = QH // KVH
EPS_NORM = 1e-05
ROPE_BASE = 100000.0
F32 = jnp.float32
BF16 = jnp.bfloat16


def dot(left, right, dims):
    return lax.dot_general(left, right, ((dims[:1], dims[1:]), ((), ())), preferred_element_type=F32)


def exchange(block, axis, distance):
    size = lax.axis_size(axis)
    return lax.ppermute(block, axis, [(i, i ^ distance) for i in range(size)])


def norm_rows(values, gain):
    return values * lax.rsqrt(jnp.mean(values * values, -1, keepdims=True) + EPS_NORM) * gain


def norm_back(values, gain, grad):
    scale = lax.rsqrt(jnp.mean(values * values, -1, keepdims=True) + EPS_NORM)
    unit = values * scale
    pulled = grad * gain
    back = scale * (pulled - unit * jnp.mean(pulled * unit, -1, keepdims=True))
    return back, jnp.sum(grad * unit, 0)


def rope(heads, cos, sin):
    half = HD // 2
    front, back = heads[:, :half], heads[:, half:]
    return jnp.concatenate([front * cos - back * sin, back * cos + front * sin], 1)


def allowed_keys(start_ref, pos_ref, kpos_ref):
    kpos = kpos_ref[...]
    return (kpos >= start_ref[...]) & (kpos <= pos_ref[...])


def attend_kernel(q_ref, k_ref, v_ref, start_ref, pos_ref, kpos_ref, o_ref, lse_ref):
    scores = dot(k_ref[0], q_ref[0], (0, 0))
    scores = jnp.where(allowed_keys(start_ref, pos_ref, kpos_ref), scores, -1e30)
    highest = jnp.max(scores, 0, keepdims=True)
    raised = jnp.exp(scores - highest)
    totals = jnp.sum(raised, 0, keepdims=True)
    weights = (raised * (1.0 / totals)).astype(BF16)
    o_ref[0] = dot(v_ref[0], weights, (1, 0)).astype(BF16)
    lse_ref[0] = highest + jnp.log(totals)


def attend_back_kernel(
    q_ref, k_ref, v_ref, start_ref, pos_ref, kpos_ref, lse_ref, do_ref, dq_ref, dk_ref, dv_ref
):
    query, key, grad_out = q_ref[0], k_ref[0], do_ref[0]
    scores = dot(key, query, (0, 0))
    scores = jnp.where(allowed_keys(start_ref, pos_ref, kpos_ref), scores, -1e30)
    weights = jnp.exp(scores - lse_ref[0])
    grad_weights = dot(v_ref[0], grad_out, (0, 0))
    row = jnp.sum(weights * grad_weights, 0, keepdims=True)
    grad_scores = (weights * (grad_weights - row)).astype(BF16)
    dq_ref[0] = dot(key, grad_scores, (1, 0)) * (HD**-0.5)
    grad_key = dot(query, grad_scores, (1, 1))
    grad_value = dot(grad_out, weights.astype(BF16), (1, 1))
    first = pl.program_id(0) % GROUP == 0

    @pl.when(first)
    def _():
        dk_ref[0] = grad_key
        dv_ref[0] = grad_value

    @pl.when(jnp.logical_not(first))
    def _():
        dk_ref[0] += grad_key
        dv_ref[0] += grad_value


def head_spec(rows, columns, index):
    return pl.BlockSpec((1, rows, columns), index)


def whole_spec(array):
    return pl.BlockSpec(array.shape, lambda h: (0,) * array.ndim)


def attention_specs(queries, keys_values, marks):
    rows, length = queries.shape[2], keys_values.shape[2]
    return [
        head_spec(HD, rows, lambda h: (h, 0, 0)),
        head_spec(HD, length, lambda h: (h // GROUP, 0, 0)),
        head_spec(HD, length, lambda h: (KVH + h // GROUP, 0, 0)),
    ] + [whole_spec(mark) for mark in marks]


PARAMS = pltpu.CompilerParams(vmem_limit_bytes=48 * 1024 * 1024)


def attend(queries, keys_values, marks):
    rows, length = queries.shape[2], keys_values.shape[2]
    return pl.pallas_call(
        attend_kernel,
        grid=(QH,),
        in_specs=attention_specs(queries, keys_values, marks),
        out_specs=[
            head_spec(HD, rows, lambda h: (h, 0, 0)),
            head_spec(1, rows, lambda h: (h, 0, 0)),
        ],
        out_shape=[
            jax.ShapeDtypeStruct((QH, HD, rows), BF16),
            jax.ShapeDtypeStruct((QH, 1, rows), F32),
        ],
        compiler_params=PARAMS,
        cost_estimate=pl.CostEstimate(
            flops=4 * QD * rows * length, bytes_accessed=2 * 2**20, transcendentals=QH * rows * length
        ),
        name="attend",
    )(queries, keys_values, keys_values, *marks)


def attend_back(queries, keys_values, marks, lse, grad_out):
    rows, length = queries.shape[2], keys_values.shape[2]
    return pl.pallas_call(
        attend_back_kernel,
        grid=(QH,),
        in_specs=attention_specs(queries, keys_values, marks)
        + [
            head_spec(1, rows, lambda h: (h, 0, 0)),
            head_spec(HD, rows, lambda h: (h, 0, 0)),
        ],
        out_specs=[
            head_spec(HD, rows, lambda h: (h, 0, 0)),
            head_spec(HD, length, lambda h: (h // GROUP, 0, 0)),
            head_spec(HD, length, lambda h: (h // GROUP, 0, 0)),
        ],
        out_shape=[
            jax.ShapeDtypeStruct((QH, HD, rows), F32),
            jax.ShapeDtypeStruct((KVH, HD, length), F32),
            jax.ShapeDtypeStruct((KVH, HD, length), F32),
        ],
        compiler_params=PARAMS,
        cost_estimate=pl.CostEstimate(
            flops=10 * QD * rows * length, bytes_accessed=4 * 2**20, transcendentals=QH * rows * length
        ),
        name="attend_back",
    )(queries, keys_values, keys_values, *marks, lse, grad_out)


def layer_forward(activation, weights, gains, cos, sin, marks):
    qkv_weight, output_weight, gate_up, down_weight = weights
    rows = activation.shape[0]
    fsdp = lax.axis_size("fsdp")
    normed = norm_rows(activation, gains[0]).astype(BF16)
    heads = dot(qkv_weight, normed, (0, 1)).reshape(QH + 2 * KVH, HD, rows)
    queries = (rope(heads[:QH], cos, sin).astype(BF16) * (HD**-0.5)).astype(BF16)
    mine = jnp.concatenate(
        [rope(heads[QH : QH + KVH], cos, sin).astype(BF16), heads[QH + KVH :].astype(BF16)], 0
    )
    keys_values = jnp.concatenate(
        [mine] + [exchange(mine, "fsdp", d) for d in range(1, fsdp)], 2
    )
    attended, lse = attend(queries, keys_values, marks)
    attended = attended.reshape(QD, rows)
    middle = activation + dot(attended, output_weight, (0, 0))
    normed_mid = norm_rows(middle, gains[1]).astype(BF16)
    both = dot(normed_mid, gate_up, (1, 0))
    half = both.shape[1] // 2
    gate, lift = both[:, :half], both[:, half:]
    hidden = (gate * jax.nn.sigmoid(gate) * lift).astype(BF16)
    result = middle + dot(hidden, down_weight, (1, 0))
    kept = (activation, normed, queries, keys_values, lse, attended, middle, normed_mid, both, hidden)
    return result, kept


def layer_backward(grad, kept, weights, gains, cos, sin, marks):
    qkv_weight, output_weight, gate_up, down_weight = weights
    activation, normed, queries, keys_values, lse, attended, middle, normed_mid, both, hidden = kept
    rows = activation.shape[0]
    fsdp = lax.axis_size("fsdp")
    half = both.shape[1] // 2
    gate, lift = both[:, :half], both[:, half:]
    branch = grad.astype(BF16)
    down_grad = dot(hidden, branch, (0, 0)).astype(BF16)
    hidden_grad = dot(branch, down_weight, (1, 1))
    sigma = jax.nn.sigmoid(gate)
    both_grad = jnp.concatenate(
        [
            (hidden_grad * lift * sigma * (1.0 + gate * (1.0 - sigma))).astype(BF16),
            (hidden_grad * gate * sigma).astype(BF16),
        ],
        1,
    )
    gate_up_grad = dot(normed_mid, both_grad, (0, 0)).astype(BF16)
    back, feedforward_gain_grad = norm_back(middle, gains[1], dot(both_grad, gate_up, (1, 1)))
    middle_grad = grad + back
    mid_branch = middle_grad.astype(BF16)
    output_grad = dot(attended, mid_branch, (1, 0)).astype(BF16)
    heads_grad = dot(output_weight, mid_branch, (1, 1)).astype(BF16).reshape(QH, HD, rows)
    dq, dk, dv = attend_back(queries, keys_values, marks, lse, heads_grad)
    parts = jnp.concatenate([dk, dv], 0).astype(BF16)
    pieces = [parts[:, :, d * rows : (d + 1) * rows] for d in range(fsdp)]
    summed = pieces[0].astype(F32)
    for d in range(1, fsdp):
        summed = summed + exchange(pieces[d], "fsdp", d).astype(F32)
    turned = rope(jnp.concatenate([dq, summed[:KVH]], 0), cos, -sin)
    raw = jnp.concatenate([turned, summed[KVH:]], 0).astype(BF16).reshape(QD + 2 * KD, rows)
    qkv_grad = dot(normed, raw, (0, 1)).astype(BF16)
    normed_grad = dot(raw, qkv_weight, (0, 1))
    back, attention_gain_grad = norm_back(activation, gains[0], normed_grad)
    return (
        middle_grad + back,
        (qkv_grad, output_grad, gate_up_grad, down_grad),
        jnp.stack([attention_gain_grad, feedforward_gain_grad]),
    )


def reduce_grads(grads, on_first):
    qkv_grad, output_grad, gate_up_grad, down_grad = grads
    fsdp, rep = lax.axis_size("fsdp"), lax.axis_size("rep")
    rows = qkv_grad.shape[0] // fsdp
    wide = gate_up_grad.shape[1]
    rest = jnp.concatenate(
        [qkv_grad, output_grad, down_grad.reshape(rows * fsdp, wide // 2)], 1
    )
    mine = jnp.where(on_first, gate_up_grad, rest)
    other = exchange(jnp.where(on_first, rest, gate_up_grad), "section", 1)
    total = (mine.astype(F32) + other.astype(F32)).astype(BF16)
    total = jnp.transpose(total.reshape(fsdp, rows, rep, wide // rep), (0, 2, 1, 3))
    for axis, size in (("fsdp", fsdp), ("rep", rep)):
        me = lax.axis_index(axis)
        own = lax.dynamic_index_in_dim(total, me, 0, keepdims=False).astype(F32)
        for d in range(1, size):
            piece = lax.dynamic_index_in_dim(total, me ^ d, 0, keepdims=False)
            own = own + exchange(piece, axis, d).astype(F32)
        total = own.astype(BF16)
    return lax.all_gather(total, "rep", axis=1, tiled=True)


def body(inputs, cotangent, segments, *shards):
    query, key, value, output, gate, up, down = [shard[0] for shard in shards[:7]]
    section = lax.axis_index("section")
    on_first = section == 0
    fsdp = lax.axis_size("fsdp")
    me = lax.axis_index("fsdp")
    rows, width = inputs.shape[2], inputs.shape[3]
    depth, wide = gate.shape[0], 2 * gate.shape[1]

    first_part = jnp.concatenate([gate, up], 1)
    second_part = jnp.concatenate([query, key, value, output, down.reshape(depth, wide // 2)], 1)
    swapped = exchange(jnp.where(on_first, second_part, first_part), "section", 1)
    shares = (
        jnp.where(on_first, first_part, swapped),
        jnp.where(on_first, swapped, second_part),
    )
    gain_shard = jnp.concatenate(shards[7:9], 0)
    gains = lax.all_gather(gain_shard, ("section", "fsdp"), axis=0)
    gains = jnp.transpose(gains.reshape(2, fsdp, 2, depth), (0, 2, 1, 3))
    gains = gains.reshape(2, 2, width).astype(F32)
    weights = []
    for share in shares:
        full = lax.all_gather(share, "fsdp", axis=0, tiled=True)
        other = exchange(full, "section", 1)
        gate_up = jnp.where(on_first, full, other)
        rest = jnp.where(on_first, other, full)
        qkv = QD + 2 * KD
        weights.append(
            (
                rest[:, :qkv],
                rest[:, qkv : qkv + width],
                gate_up,
                rest[:, qkv + width :].reshape(-1, width),
            )
        )

    segment_ids = lax.dynamic_index_in_dim(segments[:, 0], section, 0, keepdims=False)
    activation = lax.dynamic_index_in_dim(inputs[:, 0], section, 0, keepdims=False).astype(F32)
    upstream = lax.dynamic_index_in_dim(cotangent[:, 0], section, 0, keepdims=False).astype(F32)
    own_ids = lax.dynamic_slice_in_dim(segment_ids, me * rows, rows, 0)
    start = jnp.sum((segment_ids[:, None] < own_ids[None, :]).astype(jnp.int32), 0)
    places = jnp.arange(rows, dtype=jnp.int32)
    pos = me * rows + places
    key_pos = jnp.concatenate([(me ^ d) * rows + places for d in range(fsdp)])
    marks = (start[None, :], pos[None, :], key_pos[:, None])
    freqs = jnp.power(ROPE_BASE, -(jnp.arange(HD // 2, dtype=F32) * 2.0) / HD)
    angle = freqs[:, None] * (pos - start).astype(F32)[None, :]
    cos, sin = jnp.cos(angle), jnp.sin(angle)

    result, kept0 = layer_forward(activation, weights[0], gains[0], cos, sin, marks)
    handed = result.astype(BF16)
    result, kept1 = layer_forward(handed.astype(F32), weights[1], gains[1], cos, sin, marks)
    final = result.astype(BF16)

    def sorted_out(first, second, send_first, send_second):
        received = exchange(jnp.where(on_first, send_second, send_first), "section", 1)
        received = received.astype(first.dtype)
        both = [jnp.where(on_first, first, received), jnp.where(on_first, received, second)]
        return jnp.stack(both)[None, :, None]

    section_output = sorted_out(handed, final, handed, final)
    grad, grads1, gain_grads1 = layer_backward(
        upstream, kept1, weights[1], gains[1], cos, sin, marks
    )
    part1 = reduce_grads(grads1, on_first)
    returned = grad.astype(BF16)
    grad, grads0, gain_grads0 = layer_backward(
        returned.astype(F32), kept0, weights[0], gains[0], cos, sin, marks
    )
    part0 = reduce_grads(grads0, on_first)
    input_grad = sorted_out(grad, returned.astype(F32), grad.astype(BF16), returned)

    other = exchange(jnp.where(on_first, part1, part0), "section", 1)
    gate_up_grad = jnp.where(on_first, part0, other).astype(F32)
    rest = jnp.where(on_first, other, part1).astype(F32)
    gain_grads = lax.psum(
        jnp.stack([gain_grads0, gain_grads1]), ("section", "rep", "fsdp")
    )
    gain_grads = lax.dynamic_index_in_dim(gain_grads, section, 0, keepdims=False)
    gain_grads = lax.dynamic_slice_in_dim(gain_grads, me * depth, depth, 1)
    half = wide // 2
    return (
        section_output,
        input_grad,
        rest[None, :, :QD],
        rest[None, :, QD : QD + KD],
        rest[None, :, QD + KD : QD + 2 * KD],
        rest[None, :, QD + 2 * KD : half],
        gate_up_grad[None, :, :half],
        gate_up_grad[None, :, half:],
        rest[:, half:].reshape(1, -1, width),
        gain_grads[:1],
        gain_grads[1:],
    )


def solution(mesh):
    rows = P("section", "fsdp", None)
    tokens = P("section", None, "rep", "fsdp", None)
    vector = P("section", "fsdp")
    return jax.shard_map(
        body,
        mesh=mesh,
        in_specs=(P(None, "rep", "fsdp", None),) * 2
        + (P(None, "rep", None),)
        + (rows,) * 7
        + (vector,) * 2,
        out_specs=(tokens,) * 2 + (rows,) * 7 + (vector,) * 2,
        check_vma=False,
    )
```

time: 1740 us -> 528 us (0.30); the launches traced: 1720 us -> 524 us
  waiting for transfers between devices: 778 us -> 160 us
  matrix products: 394 us -> 45.9 us
  loops' own time: 108 us -> 0 us
  local copies, waits for them, and re-layouts: 184 us -> 80.4 us
  Pallas kernels: 0 us -> 39.5 us
  blocking collectives: 140 us -> 103 us
  other arithmetic: 77.1 us -> 40.9 us
  starting transfers between devices: 15.7 us -> 37.9 us
    dot_general x252 -> x24, matrix products: 394 us -> 45.9 us  [dot(): lax.dot_general(left, right, ((dims[:1], dims[1:]), ((), ())), preferred_...]
    unnamed x47 -> x2, waiting for transfers between devices: 343 us -> 0.71 us
    reduce_scatter x12 -> x0, waiting for transfers between devices: 331 us -> none  [the longest x3 104 us: reduce_rows(): lax.psum_scatter(parts[5][None].astype(jnp.bfloat16), 'fsdp', scatter_dim...]
    another operation x6 -> x0, loops' own time: 108 us -> none  [the longest x3 54.8 us: attend_backward(): lax.map(one_head, (query_heads, log_totals, grad_heads, jnp.arange(query_...]
    psum x2 -> x0, waiting for transfers between devices: 101 us -> none  [the longest x1 73.4 us: body(): lax.psum(owned[0].astype(jnp.bfloat16), 'rep').astype(jnp.float32)]
    all_gather x3 -> x2, waiting for transfers between devices: 0.02 us -> 99 us  [body(): full = lax.all_gather(share, 'fsdp', axis=0, tiled=True)]
    unnamed x333 -> x148, local copies, waits for them, and re-layouts: 82.7 us -> 13.7 us
    dynamic_slice x86 -> x4, local copies, waits for them, and re-layouts: 65.1 us -> 5.41 us  [the longest x2 5.33 us: reduce_grads(): own = lax.dynamic_index_in_dim(total, me, 0, keepdims=False).astype(F32)]
  transfers between devices with their start and end apart: 36 -> 34, of which waited for: 28 -> 10; matrix products, arithmetic and copies ran while one was open for 11% -> 22% of each run, Pallas kernels for 0% -> 0%
where the time goes in v1:
time: 528 us; the launch traced here: 524 us
  waiting for transfers between devices  160 us (30%)
  blocking collectives  103 us (20%)
  local copies, waits for them, and re-layouts  80.4 us (15%)
  matrix products  45.9 us (9%)
  other arithmetic  40.9 us (8%)
  Pallas kernels  39.5 us (7%)
  starting transfers between devices  37.9 us (7%)
  between operations  15.6 us (3%)
    all_gather x2, waiting for transfers between devices, body(): full = lax.all_gather(share, 'fsdp', axis=0, tiled=True)  99 us
    ppermute x32, waiting for transfers between devices, exchange(): return lax.ppermute(block, axis, [(i, i ^ distance) for i in range(size)])  60.8 us
    all_gather x2, blocking collectives, reduce_grads(): return lax.all_gather(total, 'rep', axis=1, tiled=True)  51 us
    dot_general x24, matrix products, dot(): lax.dot_general(left, right, ((dims[:1], dims[1:]), ((), ())), preferred_...  45.9 us
    psum x1, blocking collectives, body(): lax.psum(jnp.stack([gain_grads0, gain_grads1]), ('section', 'rep', 'fsdp'))  38.5 us
    ppermute x32, starting transfers between devices, exchange(): return lax.ppermute(block, axis, [(i, i ^ distance) for i in range(size)])  37.8 us
    pallas_call x2, Pallas kernels, attend_back(): pl.pallas_call(attend_back_kernel, grid=(QH,), in_specs=attention_specs(q...  22.9 us
    pallas_call x2, Pallas kernels, attend(): pl.pallas_call(attend_kernel, grid=(QH,), in_specs=attention_specs(querie...  16.6 us
  transfers between devices with their start and end apart: 34, of which 10 were waited for; matrix products, arithmetic and copies ran while one was open for 22% of the time, Pallas kernels for 0%

profile of v1, /device:TPU:0, one launch (start us, length us, event | category | flops | bytes accessed | tf_op | source)
XLA Modules:
  0.0 523.6 jit_solution(12474575580013346729)
XLA Ops:
  15.2 49.3 %all-gather.5.cloned.1.call-done = bf16[576,3072]{1,0:T(8,128)(2,1)} async-done(((bf16[144,3072]{1,0:T(8,128)(2,1)}), bf16[576,3072]{1,0:T(8,128)(2,1)}) %all-gather.5.cloned.1.call-update) | async-done | bytes 3538960 | tf_op jit(solution)/shard_map/all_gather | solution.py:273
  64.4 49.7 %all-gather.7.cloned.1.call-done = bf16[576,3072]{1,0:T(8,128)(2,1)} async-done(((bf16[144,3072]{1,0:T(8,128)(2,1)}), bf16[576,3072]{1,0:T(8,128)(2,1)}) %all-gather.7.cloned.1.call-update) | async-done | bytes 3538960 | tf_op jit(solution)/shard_map/all_gather | solution.py:273
  114.2 13.5 %all-gather.1 = bf16[8,2,144]{2,1,0:T(2,128)(2,1)S(1)} all-gather(bf16[1,2,144]{2,1,0:T(2,128)(2,1)S(1)} %maximum_bitcast_fusion.4), channel_id=2, replica_groups=mesh['section'=2,'rep'=4,'fsdp'=4] {'section','fsdp'}, dimensions={0}, use_global_device_ids=true | all-gather | bytes 5184 | tf_op jit(solution)/shard_map/all_gather | solution.py:268
  136.6 4.5 broadcast_select_fusion.3
  141.3 3.9 reshape.281
  146.7 3.9 reshape.283
  151.8 8.2 %attend.2 = (bf16[9,64,256]{2,1,0:T(8,128)(2,1)S(1)}, f32[9,1,256]{2,1,0:T(1,128)S(1)}) custom-call(bf16[9,64,256]{2,1,0:T(8,128)(2,1)S(1)} %maximum_multiply_fusion.q_ref, bf16[6,64,1024]{2,1,0:T(8,128)(2,1)S(1)} %pad_maximum_fusion.7.k_ref.v_ref, bf16[6,64,1024]{2,1,0:T(8,128)(2,1)S(1)} %pad_maximum_fusion.7.k_ref.v_ref, s32[1,256]{1,0:T(1,128)S(1)} %bitcast.203, ...), custom_call_target="tpu_custom_call" | custom-call | flops 603979776 | bytes 2097152 | tf_op jit(solution)/shard_map/attend/pallas_call | solution.py:113
  173.6 4.1 collective-permute-done.6
  180.8 8.4 %attend.3 = (bf16[9,64,256]{2,1,0:T(8,128)(2,1)S(1)}, f32[9,1,256]{2,1,0:T(1,128)S(1)}) custom-call(bf16[9,64,256]{2,1,0:T(8,128)(2,1)S(1)} %maximum_multiply_fusion.1.q_ref, bf16[6,64,1024]{2,1,0:T(8,128)(2,1)S(1)} %pad_maximum_fusion.8.k_ref.v_ref, bf16[6,64,1024]{2,1,0:T(8,128)(2,1)S(1)} %pad_maximum_fusion.8.k_ref.v_ref, s32[1,256]{1,0:T(1,128)S(1)} %bitcast.204, ...), custom_call_target="tpu_custom_call" | custom-call | flops 603979776 | bytes 2097152 | tf_op jit(solution)/shard_map/attend/pallas_call | solution.py:113
  196.4 11.4 %attend_back.2 = (f32[9,64,256]{2,1,0:T(8,128)S(1)}, f32[3,64,1024]{2,1,0:T(8,128)S(1)}, f32[3,64,1024]{2,1,0:T(8,128)S(1)}) custom-call(bf16[9,64,256]{2,1,0:T(8,128)(2,1)S(1)} %maximum_multiply_fusion.1.q_ref, bf16[6,64,1024]{2,1,0:T(8,128)(2,1)S(1)} %pad_maximum_fusion.8.k_ref.v_ref, bf16[6,64,1024]{2,1,0:T(8,128)(2,1)S(1)} %pad_maximum_fusion.8.k_ref.v_ref, ...), custom_call_target="tpu_custom_call" | custom-call | flops 1509949440 | bytes 4194304 | tf_op jit(solution)/shard_map/attend_back/pallas_call | solution.py:135
  214.9 3.9 copy.81
  218.8 5.5 %reshape.286 = bf16[576,1536]{1,0:T(8,128)(2,1)} reshape(bf16[1536,576]{1,0:T(8,128)(2,1)} %copy.81) | data formatting | bytes 3538944 | tf_op jit(solution)/shard_map/reshape | solution.py:235
  241.1 11.5 %attend_back.3 = (f32[9,64,256]{2,1,0:T(8,128)S(1)}, f32[3,64,1024]{2,1,0:T(8,128)S(1)}, f32[3,64,1024]{2,1,0:T(8,128)S(1)}) custom-call(bf16[9,64,256]{2,1,0:T(8,128)(2,1)S(1)} %maximum_multiply_fusion.q_ref, bf16[6,64,1024]{2,1,0:T(8,128)(2,1)S(1)} %pad_maximum_fusion.7.k_ref.v_ref, bf16[6,64,1024]{2,1,0:T(8,128)(2,1)S(1)} %pad_maximum_fusion.7.k_ref.v_ref, ...), custom_call_target="tpu_custom_call" | custom-call | flops 1509949440 | bytes 4194304 | tf_op jit(solution)/shard_map/attend_back/pallas_call | solution.py:135
  257.1 6.8 %concatenate.102 = bf16[576,3072]{1,0:T(8,128)(2,1)} concatenate(bf16[576,960]{1,0:T(8,128)(2,1)} %convolution_convert_fusion.5, bf16[576,576]{1,0:T(8,128)(2,1)} %convolution_convert_fusion.7, bf16[576,1536]{1,0:T(8,128)(2,1)} %reshape.286), dimensions={1} | concatenate | bytes 7077888 | tf_op jit(solution)/shard_map/concatenate | solution.py:234
  263.9 6.5 %broadcast_select_fusion.1 = (bf16[576,3072]{1,0:T(8,128)(2,1)}, bf16[576,3072]{1,0:T(8,128)(2,1)}) fusion(bf16[576,3072]{1,0:T(8,128)(2,1)} %concatenate.102, pred[]{:T(512)S(6)} %eq.3, bf16[256,1536]{1,0:T(8,128)(2,1)} %copy-done.52, bf16[256,1536]{1,0:T(8,128)(2,1)} %copy-done.51, f32[256,576]{0,1:T(8,128)S(1)} %copy-done.13, ...), kind=kOutput, calls=%fused_computation.5 | convolution fusion | flops 913096704 | bytes 12782849 | tf_op jit(solution)/shard_map/dot_general | solution.py:23
  273.5 3.9 copy.86
  277.4 5.1 reshape.288
  287.5 5.2 concatenate.103
  292.8 6.9 %broadcast_select_fusion = (bf16[576,3072]{1,0:T(8,128)(2,1)}, bf16[576,3072]{1,0:T(8,128)(2,1)}) fusion(bf16[576,3072]{1,0:T(8,128)(2,1)S(1)} %concatenate.103, pred[]{:T(512)S(6)} %eq.3, bf16[256,1536]{1,0:T(8,128)(2,1)} %copy-done.54, bf16[256,1536]{1,0:T(8,128)(2,1)} %copy-done.53, f32[256,576]{0,1:T(8,128)} %copy-done.15, ...), kind=kOutput, calls=%fused_computation.4 | convolution fusion | flops 913096704 | bytes 12782849 | tf_op jit(solution)/shard_map/dot_general | solution.py:23
  303.3 3.5 collective-permute-done.9
  308.7 7.0 %add_convert_fusion.1 = bf16[576,3072]{1,0:T(8,128)(2,1)} fusion(bf16[576,3072]{1,0:T(8,128)(2,1)} %collective-permute-done.17, bf16[576,3072]{1,0:T(8,128)(2,1)} %get-tuple-element.158, bf16[576,3072]{1,0:T(8,128)(2,1)S(1)} %copy-done.2, pred[]{:T(512)S(6)} %eq.3), kind=kLoop, calls=%fused_computation.1 | loop fusion | flops 8847360 | bytes 14155777 | tf_op jit(solution)/shard_map/convert_element_type | solution.py:239
  315.7 6.4 %reshape.287 = bf16[4,144,4,768]{3,2,1,0:T(4,128)(2,1)S(1)} reshape(bf16[576,3072]{1,0:T(8,128)(2,1)} %add_convert_fusion.1) | data formatting | bytes 7077888 | tf_op jit(solution)/shard_map/reshape | solution.py:240
  330.7 3.5 add_convert_fusion
  334.3 4.5 reshape.289
  344.5 3.7 collective-permute-done.18
  351.5 18.3 %collective-permute-done.19 = bf16[4,144,768]{2,1,0:T(8,128)(2,1)} collective-permute-done((bf16[4,144,768]{2,1,0:T(8,128)(2,1)}, bf16[4,144,768]{2,1,0:T(8,128)(2,1)}, u32[]{:S(2)}, u32[]{:S(2)}) %collective-permute-start.19) | collective-permute-done | bytes 884768 | tf_op jit(solution)/shard_map/ppermute | solution.py:28
  376.0 10.0 %collective-permute-done.25 = bf16[4,144,768]{2,1,0:T(8,128)(2,1)S(1)} collective-permute-done((bf16[4,144,768]{2,1,0:T(8,128)(2,1)S(1)}, bf16[4,144,768]{2,1,0:T(8,128)(2,1)S(1)}, u32[]{:S(2)}, u32[]{:S(2)}) %collective-permute-start.25) | collective-permute-done | bytes 884768 | tf_op jit(solution)/shard_map/ppermute | solution.py:28
  386.0 3.3 collective-permute-start.23
  389.3 16.1 %collective-permute-done.26 = bf16[4,144,768]{2,1,0:T(8,128)(2,1)S(1)} collective-permute-done((bf16[4,144,768]{2,1,0:T(8,128)(2,1)S(1)}, bf16[4,144,768]{2,1,0:T(8,128)(2,1)S(1)}, u32[]{:S(2)}, u32[]{:S(2)}) %collective-permute-start.26) | collective-permute-done | bytes 884768 | tf_op jit(solution)/shard_map/ppermute | solution.py:28
  410.4 33.5 %all_gather.22 = bf16[144,3072]{1,0:T(8,128)(2,1)S(1)} all-gather(bf16[144,768]{1,0:T(8,128)(2,1)S(1)} %fusion.58), channel_id=1, replica_groups=mesh['section'=2,'rep'=4,'fsdp'=4] {'rep'}, dimensions={1}, use_global_device_ids=true | all-gather | bytes 1105920 | tf_op jit(solution)/shard_map/all_gather | solution.py:248
  444.0 17.5 %all_gather.23 = bf16[144,3072]{1,0:T(8,128)(2,1)S(1)} all-gather(bf16[144,768]{1,0:T(8,128)(2,1)S(1)} %fusion.55), channel_id=1, replica_groups=mesh['section'=2,'rep'=4,'fsdp'=4] {'rep'}, dimensions={1}, use_global_device_ids=true | all-gather | bytes 1105920 | tf_op jit(solution)/shard_map/all_gather | solution.py:248
  464.0 38.5 %psum.7 = f32[2,2,576]{2,1,0:T(2,128)} all-reduce(f32[2,2,576]{2,1,0:T(2,128)} %pad_maximum_fusion.16), channel_id=1, replica_groups=mesh['section'=2,'rep'=4,'fsdp'=4] {'section','rep','fsdp'}, use_global_device_ids=true, to_apply=%region_13.14 | all-reduce | flops 2304 | bytes 18432 | tf_op jit(solution)/shard_map/psum | solution.py:326
  (327 shorter events, 129.8 us)
Async XLA Ops:
  7.2 57.2 %all-gather.5.cloned.1.call-start = ((), (), s32[]{:S(2)}) async-start(), calls=%async_computation | async-start | bytes 4423680 | tf_op jit(solution)/shard_map/all_gather | solution.py:273
  14.4 99.7 %all-gather.7.cloned.1.call-start = ((), (), s32[]{:S(2)}) async-start(), calls=%async_computation.1 | async-start | bytes 4423680 | tf_op jit(solution)/shard_map/all_gather | solution.py:273
  64.4 64.4 %collective-permute-start.1 = (bf16[576,3072]{1,0:T(8,128)(2,1)}, bf16[576,3072]{1,0:T(8,128)(2,1)}, u32[]{:S(2)}, u32[]{:S(2)}) collective-permute-start(bf16[576,3072]{1,0:T(8,128)(2,1)} %all-gather.5.cloned.1.call-done), channel_id=1, source_target_pairs={{0,16},{16,0},{1,17},{17,1},{2,18},{18,2},{3,19},{19,3},{4,20},{20... | collective-permute-start | bytes 10616840 | tf_op jit(solution)/shard_map/ppermute | solution.py:28
  114.1 22.4 %collective-permute-start.5 = (bf16[576,3072]{1,0:T(8,128)(2,1)}, bf16[576,3072]{1,0:T(8,128)(2,1)}, u32[]{:S(2)}, u32[]{:S(2)}) collective-permute-start(bf16[576,3072]{1,0:T(8,128)(2,1)} %all-gather.7.cloned.1.call-done), channel_id=1, source_target_pairs={{0,16},{16,0},{1,17},{17,1},{2,18},{18,2},{3,19},{19,3},{4,20},{20... | collective-permute-start | bytes 10616840 | tf_op jit(solution)/shard_map/ppermute | solution.py:28
  132.7 18.0 %collective-permute-start.2 = (bf16[6,64,256]{2,1,0:T(8,128)(2,1)}, bf16[6,64,256]{2,1,0:T(8,128)(2,1)S(1)}, u32[]{:S(2)}, u32[]{:S(2)}) collective-permute-start(bf16[6,64,256]{2,1,0:T(8,128)(2,1)} %pad_maximum_fusion.14), channel_id=1, source_target_pairs={{0,1},{1,0},{2,3},{3,2},{4,5},{5,4},{6,7},{7,6},{8,9},{9,8},{10,11... | collective-permute-start | bytes 589832 | tf_op jit(solution)/shard_map/ppermute | solution.py:28
  134.1 16.6 %collective-permute-start.3 = (bf16[6,64,256]{2,1,0:T(8,128)(2,1)}, bf16[6,64,256]{2,1,0:T(8,128)(2,1)S(1)}, u32[]{:S(2)}, u32[]{:S(2)}) collective-permute-start(bf16[6,64,256]{2,1,0:T(8,128)(2,1)} %pad_maximum_fusion.14), channel_id=1, source_target_pairs={{0,2},{1,3},{2,0},{3,1},{4,6},{5,7},{6,4},{7,5},{8,10},{9,11},{10,... | collective-permute-start | bytes 589832 | tf_op jit(solution)/shard_map/ppermute | solution.py:28
  135.6 15.1 %collective-permute-start.4 = (bf16[6,64,256]{2,1,0:T(8,128)(2,1)}, bf16[6,64,256]{2,1,0:T(8,128)(2,1)}, u32[]{:S(2)}, u32[]{:S(2)}) collective-permute-start(bf16[6,64,256]{2,1,0:T(8,128)(2,1)} %pad_maximum_fusion.14), channel_id=1, source_target_pairs={{0,3},{1,2},{2,1},{3,0},{4,7},{5,6},{6,5},{7,4},{8,11},{9,10},{10,... | collective-permute-start | bytes 589832 | tf_op jit(solution)/shard_map/ppermute | solution.py:28
  169.8 7.9 %collective-permute-start.6 = (bf16[6,64,256]{2,1,0:T(8,128)(2,1)S(1)}, bf16[6,64,256]{2,1,0:T(8,128)(2,1)S(1)}, u32[]{:S(2)}, u32[]{:S(2)}) collective-permute-start(bf16[6,64,256]{2,1,0:T(8,128)(2,1)S(1)} %pad_maximum_fusion.15), channel_id=1, source_target_pairs={{0,1},{1,0},{2,3},{3,2},{4,5},{5,4},{6,7},{7,6},{8,9},{9,8},{10,11... | collective-permute-start | bytes 589832 | tf_op jit(solution)/shard_map/ppermute | solution.py:28
  171.0 9.7 %collective-permute-start.7 = (bf16[6,64,256]{2,1,0:T(8,128)(2,1)S(1)}, bf16[6,64,256]{2,1,0:T(8,128)(2,1)S(1)}, u32[]{:S(2)}, u32[]{:S(2)}) collective-permute-start(bf16[6,64,256]{2,1,0:T(8,128)(2,1)S(1)} %pad_maximum_fusion.15), channel_id=1, source_target_pairs={{0,2},{1,3},{2,0},{3,1},{4,6},{5,7},{6,4},{7,5},{8,10},{9,11},{10,... | collective-permute-start | bytes 589832 | tf_op jit(solution)/shard_map/ppermute | solution.py:28
  172.5 8.2 %collective-permute-start.8 = (bf16[6,64,256]{2,1,0:T(8,128)(2,1)S(1)}, bf16[6,64,256]{2,1,0:T(8,128)(2,1)S(1)}, u32[]{:S(2)}, u32[]{:S(2)}) collective-permute-start(bf16[6,64,256]{2,1,0:T(8,128)(2,1)S(1)} %pad_maximum_fusion.15), channel_id=1, source_target_pairs={{0,3},{1,2},{2,1},{3,0},{4,7},{5,6},{6,5},{7,4},{8,11},{9,10},{10,... | collective-permute-start | bytes 589832 | tf_op jit(solution)/shard_map/ppermute | solution.py:28
  209.6 17.2 %collective-permute-start.10 = (bf16[6,64,256]{2,1,0:T(8,128)(2,1)}, bf16[6,64,256]{2,1,0:T(8,128)(2,1)}, u32[]{:S(2)}, u32[]{:S(2)}) collective-permute-start(bf16[6,64,256]{2,1,0:T(8,128)(2,1)} %get-tuple-element.123), channel_id=1, source_target_pairs={{0,1},{1,0},{2,3},{3,2},{4,5},{5,4},{6,7},{7,6},{8,9},{9,8},{10,11... | collective-permute-start | bytes 589832 | tf_op jit(solution)/shard_map/ppermute | solution.py:28
  211.3 15.6 %collective-permute-start.11 = (bf16[6,64,256]{2,1,0:T(8,128)(2,1)}, bf16[6,64,256]{2,1,0:T(8,128)(2,1)}, u32[]{:S(2)}, u32[]{:S(2)}) collective-permute-start(bf16[6,64,256]{2,1,0:T(8,128)(2,1)} %get-tuple-element.125), channel_id=1, source_target_pairs={{0,2},{1,3},{2,0},{3,1},{4,6},{5,7},{6,4},{7,5},{8,10},{9,11},{10,... | collective-permute-start | bytes 589832 | tf_op jit(solution)/shard_map/ppermute | solution.py:28
  212.2 14.6 %collective-permute-start.12 = (bf16[6,64,256]{2,1,0:T(8,128)(2,1)}, bf16[6,64,256]{2,1,0:T(8,128)(2,1)}, u32[]{:S(2)}, u32[]{:S(2)}) collective-permute-start(bf16[6,64,256]{2,1,0:T(8,128)(2,1)} %get-tuple-element.124), channel_id=1, source_target_pairs={{0,3},{1,2},{2,1},{3,0},{4,7},{5,6},{6,5},{7,4},{8,11},{9,10},{10,... | collective-permute-start | bytes 589832 | tf_op jit(solution)/shard_map/ppermute | solution.py:28
  253.6 30.2 %collective-permute-start.13 = (bf16[6,64,256]{2,1,0:T(8,128)(2,1)}, bf16[6,64,256]{2,1,0:T(8,128)(2,1)S(1)}, u32[]{:S(2)}, u32[]{:S(2)}) collective-permute-start(bf16[6,64,256]{2,1,0:T(8,128)(2,1)} %get-tuple-element.120), channel_id=1, source_target_pairs={{0,1},{1,0},{2,3},{3,2},{4,5},{5,4},{6,7},{7,6},{8,9},{9,8},{10,11... | collective-permute-start | bytes 589832 | tf_op jit(solution)/shard_map/ppermute | solution.py:28
  255.2 28.5 %collective-permute-start.14 = (bf16[6,64,256]{2,1,0:T(8,128)(2,1)}, bf16[6,64,256]{2,1,0:T(8,128)(2,1)}, u32[]{:S(2)}, u32[]{:S(2)}) collective-permute-start(bf16[6,64,256]{2,1,0:T(8,128)(2,1)} %get-tuple-element.122), channel_id=1, source_target_pairs={{0,2},{1,3},{2,0},{3,1},{4,6},{5,7},{6,4},{7,5},{8,10},{9,11},{10,... | collective-permute-start | bytes 589832 | tf_op jit(solution)/shard_map/ppermute | solution.py:28
  256.2 27.6 %collective-permute-start.15 = (bf16[6,64,256]{2,1,0:T(8,128)(2,1)}, bf16[6,64,256]{2,1,0:T(8,128)(2,1)}, u32[]{:S(2)}, u32[]{:S(2)}) collective-permute-start(bf16[6,64,256]{2,1,0:T(8,128)(2,1)} %get-tuple-element.121), channel_id=1, source_target_pairs={{0,3},{1,2},{2,1},{3,0},{4,7},{5,6},{6,5},{7,4},{8,11},{9,10},{10,... | collective-permute-start | bytes 589832 | tf_op jit(solution)/shard_map/ppermute | solution.py:28
  270.4 38.3 %collective-permute-start.17 = (bf16[576,3072]{1,0:T(8,128)(2,1)}, bf16[576,3072]{1,0:T(8,128)(2,1)}, u32[]{:S(2)}, u32[]{:S(2)}) collective-permute-start(bf16[576,3072]{1,0:T(8,128)(2,1)} %get-tuple-element.157), channel_id=1, source_target_pairs={{0,16},{16,0},{1,17},{17,1},{2,18},{18,2},{3,19},{19,3},{4,20},{20... | collective-permute-start | bytes 10616840 | tf_op jit(solution)/shard_map/ppermute | solution.py:28
  299.7 31.0 %collective-permute-start.24 = (bf16[576,3072]{1,0:T(8,128)(2,1)}, bf16[576,3072]{1,0:T(8,128)(2,1)}, u32[]{:S(2)}, u32[]{:S(2)}) collective-permute-start(bf16[576,3072]{1,0:T(8,128)(2,1)} %get-tuple-element.155), channel_id=1, source_target_pairs={{0,16},{16,0},{1,17},{17,1},{2,18},{18,2},{3,19},{19,3},{4,20},{20... | collective-permute-start | bytes 10616840 | tf_op jit(solution)/shard_map/ppermute | solution.py:28
  325.2 22.9 %collective-permute-start.18 = (bf16[4,144,768]{2,1,0:T(8,128)(2,1)}, bf16[4,144,768]{2,1,0:T(8,128)(2,1)}, u32[]{:S(2)}, u32[]{:S(2)}) collective-permute-start(bf16[4,144,768]{2,1,0:T(8,128)(2,1)} %bitcast.195), channel_id=1, source_target_pairs={{0,1},{1,0},{2,3},{3,2},{4,5},{5,4},{6,7},{7,6},{8,9},{9,8},{10,11... | collective-permute-start | bytes 2654216 | tf_op jit(solution)/shard_map/ppermute | solution.py:28
  328.0 41.9 %collective-permute-start.19 = (bf16[4,144,768]{2,1,0:T(8,128)(2,1)}, bf16[4,144,768]{2,1,0:T(8,128)(2,1)}, u32[]{:S(2)}, u32[]{:S(2)}) collective-permute-start(bf16[4,144,768]{2,1,0:T(8,128)(2,1)} %bitcast.194), channel_id=1, source_target_pairs={{0,2},{1,3},{2,0},{3,1},{4,6},{5,7},{6,4},{7,5},{8,10},{9,11},{10,... | collective-permute-start | bytes 2654216 | tf_op jit(solution)/shard_map/ppermute | solution.py:28
  329.3 40.6 %collective-permute-start.20 = (bf16[4,144,768]{2,1,0:T(8,128)(2,1)}, bf16[4,144,768]{2,1,0:T(8,128)(2,1)}, u32[]{:S(2)}, u32[]{:S(2)}) collective-permute-start(bf16[4,144,768]{2,1,0:T(8,128)(2,1)} %bitcast.193), channel_id=1, source_target_pairs={{0,3},{1,2},{2,1},{3,0},{4,7},{5,6},{6,5},{7,4},{8,11},{9,10},{10,... | collective-permute-start | bytes 2654216 | tf_op jit(solution)/shard_map/ppermute | solution.py:28
  342.1 43.9 %collective-permute-start.25 = (bf16[4,144,768]{2,1,0:T(8,128)(2,1)S(1)}, bf16[4,144,768]{2,1,0:T(8,128)(2,1)S(1)}, u32[]{:S(2)}, u32[]{:S(2)}) collective-permute-start(bf16[4,144,768]{2,1,0:T(8,128)(2,1)S(1)} %bitcast.219), channel_id=1, source_target_pairs={{0,1},{1,0},{2,3},{3,2},{4,5},{5,4},{6,7},{7,6},{8,9},{9,8},{10,11... | collective-permute-start | bytes 2654216 | tf_op jit(solution)/shard_map/ppermute | solution.py:28
  344.0 61.4 %collective-permute-start.26 = (bf16[4,144,768]{2,1,0:T(8,128)(2,1)S(1)}, bf16[4,144,768]{2,1,0:T(8,128)(2,1)S(1)}, u32[]{:S(2)}, u32[]{:S(2)}) collective-permute-start(bf16[4,144,768]{2,1,0:T(8,128)(2,1)S(1)} %bitcast.217), channel_id=1, source_target_pairs={{0,2},{1,3},{2,0},{3,1},{4,6},{5,7},{6,4},{7,5},{8,10},{9,11},{10,... | collective-permute-start | bytes 2654216 | tf_op jit(solution)/shard_map/ppermute | solution.py:28
  348.1 57.3 %collective-permute-start.27 = (bf16[4,144,768]{2,1,0:T(8,128)(2,1)S(1)}, bf16[4,144,768]{2,1,0:T(8,128)(2,1)S(1)}, u32[]{:S(2)}, u32[]{:S(2)}) collective-permute-start(bf16[4,144,768]{2,1,0:T(8,128)(2,1)S(1)} %bitcast.218), channel_id=1, source_target_pairs={{0,3},{1,2},{2,1},{3,0},{4,7},{5,6},{6,5},{7,4},{8,11},{9,10},{10,... | collective-permute-start | bytes 2654216 | tf_op jit(solution)/shard_map/ppermute | solution.py:28
  372.0 37.8 %collective-permute-start.21 = (bf16[144,768]{1,0:T(8,128)(2,1)S(1)}, bf16[144,768]{1,0:T(8,128)(2,1)S(1)}, u32[]{:S(2)}, u32[]{:S(2)}) collective-permute-start(bf16[144,768]{1,0:T(8,128)(2,1)S(1)} %get-tuple-element.111), channel_id=1, source_target_pairs={{0,4},{4,0},{8,12},{12,8},{1,5},{5,1},{9,13},{13,9},{2,6},{6,2},{1... | collective-permute-start | bytes 663560 | tf_op jit(solution)/shard_map/ppermute | solution.py:28
  373.5 36.8 %collective-permute-start.22 = (bf16[144,768]{1,0:T(8,128)(2,1)S(1)}, bf16[144,768]{1,0:T(8,128)(2,1)S(1)}, u32[]{:S(2)}, u32[]{:S(2)}) collective-permute-start(bf16[144,768]{1,0:T(8,128)(2,1)S(1)} %get-tuple-element.113), channel_id=1, source_target_pairs={{0,8},{4,12},{8,0},{12,4},{1,9},{5,13},{9,1},{13,5},{2,10},{6,14},... | collective-permute-start | bytes 663560 | tf_op jit(solution)/shard_map/ppermute | solution.py:28
  386.0 24.3 %collective-permute-start.23 = (bf16[144,768]{1,0:T(8,128)(2,1)S(1)}, bf16[144,768]{1,0:T(8,128)(2,1)S(1)}, u32[]{:S(2)}, u32[]{:S(2)}) collective-permute-start(bf16[144,768]{1,0:T(8,128)(2,1)S(1)} %get-tuple-element.112), channel_id=1, source_target_pairs={{0,12},{4,8},{8,4},{12,0},{1,13},{5,9},{9,5},{13,1},{2,14},{6,10},... | collective-permute-start | bytes 663560 | tf_op jit(solution)/shard_map/ppermute | solution.py:28
  405.8 38.0 %collective-permute-start.28 = (bf16[144,768]{1,0:T(8,128)(2,1)S(1)}, bf16[144,768]{1,0:T(8,128)(2,1)S(1)}, u32[]{:S(2)}, u32[]{:S(2)}) collective-permute-start(bf16[144,768]{1,0:T(8,128)(2,1)S(1)} %get-tuple-element.108), channel_id=1, source_target_pairs={{0,4},{4,0},{8,12},{12,8},{1,5},{5,1},{9,13},{13,9},{2,6},{6,2},{1... | collective-permute-start | bytes 663560 | tf_op jit(solution)/shard_map/ppermute | solution.py:28
  407.4 36.5 %collective-permute-start.29 = (bf16[144,768]{1,0:T(8,128)(2,1)S(1)}, bf16[144,768]{1,0:T(8,128)(2,1)S(1)}, u32[]{:S(2)}, u32[]{:S(2)}) collective-permute-start(bf16[144,768]{1,0:T(8,128)(2,1)S(1)} %get-tuple-element.110), channel_id=1, source_target_pairs={{0,8},{4,12},{8,0},{12,4},{1,9},{5,13},{9,1},{13,5},{2,10},{6,14},... | collective-permute-start | bytes 663560 | tf_op jit(solution)/shard_map/ppermute | solution.py:28
  409.8 34.1 %collective-permute-start.30 = (bf16[144,768]{1,0:T(8,128)(2,1)S(1)}, bf16[144,768]{1,0:T(8,128)(2,1)S(1)}, u32[]{:S(2)}, u32[]{:S(2)}) collective-permute-start(bf16[144,768]{1,0:T(8,128)(2,1)S(1)} %get-tuple-element.109), channel_id=1, source_target_pairs={{0,12},{4,8},{8,4},{12,0},{1,13},{5,9},{9,5},{13,1},{2,14},{6,10},... | collective-permute-start | bytes 663560 | tf_op jit(solution)/shard_map/ppermute | solution.py:28
  462.6 44.0 %collective-permute-start.31 = (bf16[144,3072]{1,0:T(8,128)(2,1)}, bf16[144,3072]{1,0:T(8,128)(2,1)}, u32[]{:S(2)}, u32[]{:S(2)}) collective-permute-start(bf16[144,3072]{1,0:T(8,128)(2,1)} %broadcast_select_fusion.10), channel_id=1, source_target_pairs={{0,16},{16,0},{1,17},{17,1},{2,18},{18,2},{3,19},{19,3},{4,20},{20... | collective-permute-start | bytes 2654216 | tf_op jit(solution)/shard_map/ppermute | solution.py:28
  462.8 41.1 %collective-permute-start.16 = (bf16[256,576]{0,1:T(8,128)(2,1)S(1)}, bf16[256,576]{0,1:T(8,128)(2,1)}, u32[]{:S(2)}, u32[]{:S(2)}) collective-permute-start(bf16[256,576]{0,1:T(8,128)(2,1)S(1)} %convert_select_fusion.2), channel_id=1, source_target_pairs={{0,16},{16,0},{1,17},{17,1},{2,18},{18,2},{3,19},{19,3},{4,20},{20... | collective-permute-start | bytes 884744 | tf_op jit(solution)/shard_map/ppermute | solution.py:28
  (73 other events, 1329.1 us)
Sparse Core Ops, SparseCore 0:
  14.5 49.8 all-gather.4
  66.9 47.2 all-gather.6

commit v2 on v1

--- a/solution.py
+++ b/solution.py
@@ -1,5 +1,3 @@
-import functools
-
 import jax
 import jax.numpy as jnp
 from jax import lax
@@ -175,40 +173,34 @@
     attended = attended.reshape(QD, rows)
     middle = activation + dot(attended, output_weight, (0, 0))
     normed_mid = norm_rows(middle, gains[1]).astype(BF16)
-    both = dot(normed_mid, gate_up, (1, 0))
-    half = both.shape[1] // 2
-    gate, lift = both[:, :half], both[:, half:]
+    gate, lift = [dot(normed_mid, weight, (1, 0)) for weight in gate_up]
     hidden = (gate * jax.nn.sigmoid(gate) * lift).astype(BF16)
     result = middle + dot(hidden, down_weight, (1, 0))
-    kept = (activation, normed, queries, keys_values, lse, attended, middle, normed_mid, both, hidden)
+    kept = (activation, normed, queries, keys_values, lse, attended, middle, normed_mid, gate, lift, hidden)
     return result, kept
 
 
-def layer_backward(grad, kept, weights, gains, cos, sin, marks):
-    qkv_weight, output_weight, gate_up, down_weight = weights
-    activation, normed, queries, keys_values, lse, attended, middle, normed_mid, both, hidden = kept
-    rows = activation.shape[0]
-    fsdp = lax.axis_size("fsdp")
-    half = both.shape[1] // 2
-    gate, lift = both[:, :half], both[:, half:]
+def feedforward_back(grad, kept, weights, gains):
+    _, _, gate_up, down_weight = weights
+    middle, normed_mid, gate, lift, hidden = kept[6:]
     branch = grad.astype(BF16)
     down_grad = dot(hidden, branch, (0, 0)).astype(BF16)
     hidden_grad = dot(branch, down_weight, (1, 1))
     sigma = jax.nn.sigmoid(gate)
-    both_grad = jnp.concatenate(
-        [
-            (hidden_grad * lift * sigma * (1.0 + gate * (1.0 - sigma))).astype(BF16),
-            (hidden_grad * gate * sigma).astype(BF16),
-        ],
-        1,
-    )
-    gate_up_grad = dot(normed_mid, both_grad, (0, 0)).astype(BF16)
-    back, feedforward_gain_grad = norm_back(middle, gains[1], dot(both_grad, gate_up, (1, 1)))
-    middle_grad = grad + back
-    mid_branch = middle_grad.astype(BF16)
-    output_grad = dot(attended, mid_branch, (1, 0)).astype(BF16)
-    heads_grad = dot(output_weight, mid_branch, (1, 1)).astype(BF16).reshape(QH, HD, rows)
-    dq, dk, dv = attend_back(queries, keys_values, marks, lse, heads_grad)
+    gate_part = (hidden_grad * lift * sigma * (1.0 + gate * (1.0 - sigma))).astype(BF16)
+    lift_part = (hidden_grad * gate * sigma).astype(BF16)
+    gate_grad = dot(normed_mid, gate_part, (0, 0)).astype(BF16)
+    up_grad = dot(normed_mid, lift_part, (0, 0)).astype(BF16)
+    pulled = dot(gate_part, gate_up[0], (1, 1)) + dot(lift_part, gate_up[1], (1, 1))
+    back, gain_grad = norm_back(middle, gains[1], pulled)
+    return grad + back, gate_grad, up_grad, down_grad, gain_grad
+
+
+def projections_back(middle_grad, dq, dk, dv, kept, weights, gains, cos, sin):
+    activation, normed = kept[:2]
+    qkv_weight = weights[0]
+    rows = activation.shape[0]
+    fsdp = lax.axis_size("fsdp")
     parts = jnp.concatenate([dk, dv], 0).astype(BF16)
     pieces = [parts[:, :, d * rows : (d + 1) * rows] for d in range(fsdp)]
     summed = pieces[0].astype(F32)
@@ -217,71 +209,94 @@
     turned = rope(jnp.concatenate([dq, summed[:KVH]], 0), cos, -sin)
     raw = jnp.concatenate([turned, summed[KVH:]], 0).astype(BF16).reshape(QD + 2 * KD, rows)
     qkv_grad = dot(normed, raw, (0, 1)).astype(BF16)
-    normed_grad = dot(raw, qkv_weight, (0, 1))
-    back, attention_gain_grad = norm_back(activation, gains[0], normed_grad)
-    return (
-        middle_grad + back,
-        (qkv_grad, output_grad, gate_up_grad, down_grad),
-        jnp.stack([attention_gain_grad, feedforward_gain_grad]),
-    )
-
-
-def reduce_grads(grads, on_first):
-    qkv_grad, output_grad, gate_up_grad, down_grad = grads
-    fsdp, rep = lax.axis_size("fsdp"), lax.axis_size("rep")
-    rows = qkv_grad.shape[0] // fsdp
-    wide = gate_up_grad.shape[1]
-    rest = jnp.concatenate(
-        [qkv_grad, output_grad, down_grad.reshape(rows * fsdp, wide // 2)], 1
-    )
-    mine = jnp.where(on_first, gate_up_grad, rest)
-    other = exchange(jnp.where(on_first, rest, gate_up_grad), "section", 1)
-    total = (mine.astype(F32) + other.astype(F32)).astype(BF16)
-    total = jnp.transpose(total.reshape(fsdp, rows, rep, wide // rep), (0, 2, 1, 3))
-    for axis, size in (("fsdp", fsdp), ("rep", rep)):
-        me = lax.axis_index(axis)
-        own = lax.dynamic_index_in_dim(total, me, 0, keepdims=False).astype(F32)
-        for d in range(1, size):
-            piece = lax.dynamic_index_in_dim(total, me ^ d, 0, keepdims=False)
-            own = own + exchange(piece, axis, d).astype(F32)
-        total = own.astype(BF16)
-    return lax.all_gather(total, "rep", axis=1, tiled=True)
+    back, gain_grad = norm_back(activation, gains[0], dot(raw, qkv_weight, (0, 1)))
+    return middle_grad + back, qkv_grad, gain_grad
+
+
+def sum_section(left, right, on_first):
+    other = exchange(jnp.where(on_first, right, left), "section", 1)
+    return (jnp.where(on_first, left, right).astype(F32) + other.astype(F32)).astype(BF16)
+
+
+def sum_scatter(total, axis, dim):
+    size, me = lax.axis_size(axis), lax.axis_index(axis)
+    span = total.shape[dim] // size
+    own = lax.dynamic_slice_in_dim(total, me * span, span, dim).astype(F32)
+    for d in range(1, size):
+        piece = lax.dynamic_slice_in_dim(total, (me ^ d) * span, span, dim)
+        own = own + exchange(piece, axis, d).astype(F32)
+    return own.astype(BF16)
+
+
+def collect(share, axis, dim):
+    size, me = lax.axis_size(axis), lax.axis_index(axis)
+    span = share.shape[dim]
+    shape = list(share.shape)
+    shape[dim] = span * size
+    full = jnp.zeros(shape, share.dtype)
+    for d in range(size):
+        block = share if d == 0 else exchange(share, axis, d)
+        full = lax.dynamic_update_slice_in_dim(full, block, (me ^ d) * span, dim)
+    return full
+
+
+def tie(*arrays):
+    return lax.optimization_barrier(arrays)
 
 
 def body(inputs, cotangent, segments, *shards):
     query, key, value, output, gate, up, down = [shard[0] for shard in shards[:7]]
     section = lax.axis_index("section")
     on_first = section == 0
-    fsdp = lax.axis_size("fsdp")
+    fsdp, rep = lax.axis_size("fsdp"), lax.axis_size("rep")
     me = lax.axis_index("fsdp")
     rows, width = inputs.shape[2], inputs.shape[3]
-    depth, wide = gate.shape[0], 2 * gate.shape[1]
-
-    first_part = jnp.concatenate([gate, up], 1)
-    second_part = jnp.concatenate([query, key, value, output, down.reshape(depth, wide // 2)], 1)
-    swapped = exchange(jnp.where(on_first, second_part, first_part), "section", 1)
-    shares = (
-        jnp.where(on_first, first_part, swapped),
-        jnp.where(on_first, swapped, second_part),
-    )
+    depth, half = gate.shape
+    qkv = QD + 2 * KD
+
+    attention_shard = jnp.concatenate([query, key, value, output], 1)
+    down_shard = down.reshape(depth, half)
+    shares = []
+    for left, right in ((attention_shard, down_shard), (gate, up)):
+        swapped = exchange(jnp.where(on_first, right, left), "section", 1)
+        shares.append(
+            (jnp.where(on_first, left, swapped), jnp.where(on_first, swapped, right))
+        )
     gain_shard = jnp.concatenate(shards[7:9], 0)
-    gains = lax.all_gather(gain_shard, ("section", "fsdp"), axis=0)
-    gains = jnp.transpose(gains.reshape(2, fsdp, 2, depth), (0, 2, 1, 3))
-    gains = gains.reshape(2, 2, width).astype(F32)
+    other = exchange(gain_shard, "section", 1)
+    gain_shard = jnp.stack(
+        [jnp.where(on_first, gain_shard, other), jnp.where(on_first, other, gain_shard)]
+    )
+    gains = collect(gain_shard[None], "fsdp", 0)
+    gains = jnp.transpose(gains, (1, 2, 0, 3)).reshape(2, 2, width).astype(F32)
+
+    def both_parts(full):
+        other = exchange(full, "section", 1)
+        return jnp.where(on_first, full, other), jnp.where(on_first, other, full)
+
     weights = []
-    for share in shares:
-        full = lax.all_gather(share, "fsdp", axis=0, tiled=True)
-        other = exchange(full, "section", 1)
-        gate_up = jnp.where(on_first, full, other)
-        rest = jnp.where(on_first, other, full)
-        qkv = QD + 2 * KD
-        weights.append(
-            (
-                rest[:, :qkv],
-                rest[:, qkv : qkv + width],
-                gate_up,
-                rest[:, qkv + width :].reshape(-1, width),
-            )
+    before = None
+    for layer in range(2):
+        pairs = []
+        for kind in range(2):
+            share = shares[kind][layer]
+            if before is not None:
+                share, before = tie(share, before)
+                if kind == 1:
+                    pairs[0] = before
+                elif layer == 1:
+                    weights[0][1] = before
+            before = collect(share, "fsdp", 0)
+            pairs.append(before)
+        weights.append(pairs)
+    for layer in range(2):
+        attention, down_full = both_parts(weights[layer][0])
+        gate_full, up_full = both_parts(weights[layer][1])
+        weights[layer] = (
+            attention[:, :qkv],
+            attention[:, qkv:],
+            (gate_full, up_full),
+            down_full.reshape(-1, width),
         )
 
     segment_ids = lax.dynamic_index_in_dim(segments[:, 0], section, 0, keepdims=False)
@@ -309,38 +324,91 @@
         return jnp.stack(both)[None, :, None]
 
     section_output = sorted_out(handed, final, handed, final)
-    grad, grads1, gain_grads1 = layer_backward(
-        upstream, kept1, weights[1], gains[1], cos, sin, marks
-    )
-    part1 = reduce_grads(grads1, on_first)
+
+    def heads_back(middle_grad, kept, layer):
+        branch = middle_grad.astype(BF16)
+        output_grad = dot(kept[5], branch, (1, 0)).astype(BF16)
+        heads = dot(weights[layer][1], branch, (1, 1)).astype(BF16).reshape(QH, HD, rows)
+        return heads, output_grad
+
+    def second_chunk(qkv_grad, output_grad, down_grad):
+        return sum_section(
+            jnp.concatenate([qkv_grad, output_grad], 1),
+            down_grad.reshape(qkv_grad.shape[0], half),
+            on_first,
+        )
+
+    middle_grad, gate_grad, up_grad, down_grad, feed_gain1 = feedforward_back(
+        upstream, kept1, weights[1], gains[1]
+    )
+    heads, output_grad = heads_back(middle_grad, kept1, 1)
+    early1 = sum_section(gate_grad, up_grad, on_first)
+    dq, dk, dv = attend_back(kept1[2], kept1[3], marks, kept1[4], heads)
+    dq, dk, dv, early1 = tie(dq, dk, dv, early1)
+    grad, qkv_grad, attention_gain1 = projections_back(
+        middle_grad, dq, dk, dv, kept1, weights[1], gains[1], cos, sin
+    )
+    early1 = sum_scatter(early1, "fsdp", 0)
     returned = grad.astype(BF16)
-    grad, grads0, gain_grads0 = layer_backward(
-        returned.astype(F32), kept0, weights[0], gains[0], cos, sin, marks
-    )
-    part0 = reduce_grads(grads0, on_first)
+    late1 = second_chunk(qkv_grad, output_grad, down_grad)
+
+    middle_grad, gate_grad, up_grad, down_grad, feed_gain0 = feedforward_back(
+        returned.astype(F32), kept0, weights[0], gains[0]
+    )
+    heads, output_grad = heads_back(middle_grad, kept0, 0)
+    heads, early1, late1 = tie(heads, early1, late1)
+    early1 = sum_scatter(early1, "rep", 1)
+    late1 = sum_scatter(late1, "fsdp", 0)
+    early0 = sum_section(gate_grad, up_grad, on_first)
+    dq, dk, dv = attend_back(kept0[2], kept0[3], marks, kept0[4], heads)
+    dq, dk, dv, early0, early1 = tie(dq, dk, dv, early0, early1)
+    early1 = collect(early1, "rep", 1)
+    grad, qkv_grad, attention_gain0 = projections_back(
+        middle_grad, dq, dk, dv, kept0, weights[0], gains[0], cos, sin
+    )
+    grad, late1, early1 = tie(grad, late1, early1)
+    early0 = sum_scatter(early0, "fsdp", 0)
+    late0 = second_chunk(qkv_grad, output_grad, down_grad)
     input_grad = sorted_out(grad, returned.astype(F32), grad.astype(BF16), returned)
 
-    other = exchange(jnp.where(on_first, part1, part0), "section", 1)
-    gate_up_grad = jnp.where(on_first, part0, other).astype(F32)
-    rest = jnp.where(on_first, other, part1).astype(F32)
-    gain_grads = lax.psum(
-        jnp.stack([gain_grads0, gain_grads1]), ("section", "rep", "fsdp")
-    )
-    gain_grads = lax.dynamic_index_in_dim(gain_grads, section, 0, keepdims=False)
-    gain_grads = lax.dynamic_slice_in_dim(gain_grads, me * depth, depth, 1)
-    half = wide // 2
+    def gathered(part):
+        return collect(sum_scatter(part, "rep", 1), "rep", 1)
+
+    def owned(part0, part1):
+        other = exchange(jnp.where(on_first, part1, part0), "section", 1)
+        left = jnp.where(on_first, part0, other).astype(F32)
+        return left, jnp.where(on_first, other, part1).astype(F32)
+
+    late1 = gathered(late1)
+    early0 = gathered(early0)
+    late0 = gathered(sum_scatter(late0, "fsdp", 0))
+    gate_sum, up_sum = owned(early0, early1)
+    rest, down_sum = owned(late0, late1)
+
+    gain_grads = jnp.stack([attention_gain0, feed_gain0, attention_gain1, feed_gain1])
+    kept = jnp.where(on_first, gain_grads[:2], gain_grads[2:])
+    sent = jnp.where(on_first, gain_grads[2:], gain_grads[:2])
+    gain_grads = kept + exchange(sent, "section", 1)
+    total = gain_grads
+    gain_sum = lax.dynamic_slice_in_dim(total, me * depth, depth, 1)
+    for d in range(1, fsdp):
+        piece = lax.dynamic_slice_in_dim(total, (me ^ d) * depth, depth, 1)
+        gain_sum = gain_sum + exchange(piece, "fsdp", d)
+    total = gain_sum
+    for d in range(1, rep):
+        gain_sum = gain_sum + exchange(total, "rep", d)
     return (
         section_output,
         input_grad,
         rest[None, :, :QD],
         rest[None, :, QD : QD + KD],
-        rest[None, :, QD + KD : QD + 2 * KD],
-        rest[None, :, QD + 2 * KD : half],
-        gate_up_grad[None, :, :half],
-        gate_up_grad[None, :, half:],
-        rest[:, half:].reshape(1, -1, width),
-        gain_grads[:1],
-        gain_grads[1:],
+        rest[None, :, QD + KD : qkv],
+        rest[None, :, qkv:],
+        gate_sum[None],
+        up_sum[None],
+        down_sum.reshape(1, -1, width),
+        gain_sum[:1],
+        gain_sum[1:],
     )
 
 

time: 528 us -> 431 us (0.82)
  blocking collectives: 103 us -> 0 us
  starting transfers between devices: 37.9 us -> 85.8 us
  local copies, waits for them, and re-layouts: 80.4 us -> 58.3 us
  between operations: 15.6 us -> 2.99 us
    all_gather x2 -> x0, waiting for transfers between devices: 99 us -> none  [body(): full = lax.all_gather(share, 'fsdp', axis=0, tiled=True)]
    ppermute x32 -> x85, waiting for transfers between devices: 60.8 us -> 155 us  [exchange(): return lax.ppermute(block, axis, [(i, i ^ distance) for i in range(size)])]
    all_gather x3 -> x0, blocking collectives: 64.5 us -> none  [the longest x2 51 us: reduce_grads(): return lax.all_gather(total, 'rep', axis=1, tiled=True)]
    ppermute x32 -> x85, starting transfers between devices: 37.8 us -> 85.8 us  [exchange(): return lax.ppermute(block, axis, [(i, i ^ distance) for i in range(size)])]
    psum x1 -> x0, blocking collectives: 38.5 us -> none  [body(): lax.psum(jnp.stack([gain_grads0, gain_grads1]), ('section', 'rep', 'fsdp'))]
    concatenate x3 -> x1, local copies, waits for them, and re-layouts: 12.5 us -> 0.21 us  [body(): attention_shard = jnp.concatenate([query, key, value, output], 1)]
    reshape x7 -> x5, local copies, waits for them, and re-layouts: 31.3 us -> 19.4 us  [the longest x2 9.46 us: second_chunk(): down_grad.reshape(qkv_grad.shape[0], half)]
    dynamic_update_slice x0 -> x32, local copies, waits for them, and re-layouts: none -> 11.2 us  [collect(): full = lax.dynamic_update_slice_in_dim(full, block, (me ^ d) * span, dim)]
  transfers between devices with their start and end apart: 34 -> 85, of which waited for: 10 -> 38; matrix products, arithmetic and copies ran while one was open for 22% -> 28% of each run, Pallas kernels for 0% -> 9%
where the time goes in v2:
time: 431 us; the launch traced here: 425 us
  waiting for transfers between devices  155 us (36%)
  starting transfers between devices  85.8 us (20%)
  local copies, waits for them, and re-layouts  58.3 us (14%)
  matrix products  45.8 us (11%)
  Pallas kernels  39.7 us (9%)
  other arithmetic  37.3 us (9%)
    ppermute x85, waiting for transfers between devices, exchange(): return lax.ppermute(block, axis, [(i, i ^ distance) for i in range(size)])  155 us
    ppermute x85, starting transfers between devices, exchange(): return lax.ppermute(block, axis, [(i, i ^ distance) for i in range(size)])  85.8 us
    dot_general x30, matrix products, dot(): lax.dot_general(left, right, ((dims[:1], dims[1:]), ((), ())), preferred_...  45.8 us
    pallas_call x2, Pallas kernels, attend_back(): pl.pallas_call(attend_back_kernel, grid=(QH,), in_specs=attention_specs(q...  23.1 us
    pallas_call x2, Pallas kernels, attend(): pl.pallas_call(attend_kernel, grid=(QH,), in_specs=attention_specs(querie...  16.6 us
    dynamic_update_slice x32, local copies, waits for them, and re-layouts, collect(): full = lax.dynamic_update_slice_in_dim(full, block, (me ^ d) * span, dim)  11.2 us
    unnamed x132, local copies, waits for them, and re-layouts  10.1 us
    reshape x2, local copies, waits for them, and re-layouts, second_chunk(): down_grad.reshape(qkv_grad.shape[0], half)  9.46 us
  transfers between devices with their start and end apart: 85, of which 38 were waited for; matrix products, arithmetic and copies ran while one was open for 28% of the time, Pallas kernels for 9%

profile of v2, /device:TPU:0, one launch (start us, length us, event | category | flops | bytes accessed | tf_op | source)
XLA Modules:
  0.0 425.0 jit_solution(434062493081580478)
XLA Ops:
  14.4 8.3 %collective-permute-done.2 = bf16[144,1536]{1,0:T(8,128)(2,1)S(1)} collective-permute-done((bf16[144,1536]{1,0:T(8,128)(2,1)S(1)}, bf16[144,1536]{1,0:T(8,128)(2,1)S(1)}, u32[]{:S(2)}, u32[]{:S(2)}) %collective-permute-start.2) | collective-permute-done | bytes 442400 | tf_op jit(solution)/shard_map/ppermute | solution.py:26
  22.7 10.6 %collective-permute-done.3 = bf16[144,1536]{1,0:T(8,128)(2,1)S(1)} collective-permute-done((bf16[144,1536]{1,0:T(8,128)(2,1)S(1)}, bf16[144,1536]{1,0:T(8,128)(2,1)S(1)}, u32[]{:S(2)}, u32[]{:S(2)}) %collective-permute-start.3) | collective-permute-done | bytes 442400 | tf_op jit(solution)/shard_map/ppermute | solution.py:26
  39.1 7.5 %collective-permute-done.13 = bf16[144,1536]{1,0:T(8,128)(2,1)S(1)} collective-permute-done((bf16[144,1536]{1,0:T(8,128)(2,1)S(1)}, bf16[144,1536]{1,0:T(8,128)(2,1)S(1)}, u32[]{:S(2)}, u32[]{:S(2)}) %collective-permute-start.13) | collective-permute-done | bytes 442400 | tf_op jit(solution)/shard_map/ppermute | solution.py:26
  47.4 8.2 %collective-permute-done.14 = bf16[144,1536]{1,0:T(8,128)(2,1)S(1)} collective-permute-done((bf16[144,1536]{1,0:T(8,128)(2,1)S(1)}, bf16[144,1536]{1,0:T(8,128)(2,1)S(1)}, u32[]{:S(2)}, u32[]{:S(2)}) %collective-permute-start.14) | collective-permute-done | bytes 442400 | tf_op jit(solution)/shard_map/ppermute | solution.py:26
  61.7 5.1 %collective-permute-done.7 = bf16[1,2,2,144]{3,2,1,0:T(2,128)(2,1)S(1)} collective-permute-done((bf16[1,2,2,144]{3,2,1,0:T(2,128)(2,1)S(1)}, bf16[1,2,2,144]{3,2,1,0:T(2,128)(2,1)S(1)}, u32[]{:S(2)}, u32[]{:S(2)}) %collective-permute-start.7) | collective-permute-done | bytes 1184 | tf_op jit(solution)/shard_map/ppermute | solution.py:26
  74.1 15.0 %collective-permute-done.18 = bf16[144,1536]{1,0:T(8,128)(2,1)S(1)} collective-permute-done((bf16[144,1536]{1,0:T(8,128)(2,1)S(1)}, bf16[144,1536]{1,0:T(8,128)(2,1)S(1)}, u32[]{:S(2)}, u32[]{:S(2)}) %collective-permute-start.18) | collective-permute-done | bytes 442400 | tf_op jit(solution)/shard_map/ppermute | solution.py:26
  96.7 7.2 %collective-permute-done.24 = bf16[144,1536]{1,0:T(8,128)(2,1)S(1)} collective-permute-done((bf16[144,1536]{1,0:T(8,128)(2,1)S(1)}, bf16[144,1536]{1,0:T(8,128)(2,1)S(1)}, u32[]{:S(2)}, u32[]{:S(2)}) %collective-permute-start.24) | collective-permute-done | bytes 442400 | tf_op jit(solution)/shard_map/ppermute | solution.py:26
  104.6 10.0 %collective-permute-done.25 = bf16[144,1536]{1,0:T(8,128)(2,1)S(1)} collective-permute-done((bf16[144,1536]{1,0:T(8,128)(2,1)S(1)}, bf16[144,1536]{1,0:T(8,128)(2,1)S(1)}, u32[]{:S(2)}, u32[]{:S(2)}) %collective-permute-start.25) | collective-permute-done | bytes 442400 | tf_op jit(solution)/shard_map/ppermute | solution.py:26
  116.2 3.0 broadcast_select_fusion.8
  124.8 4.8 %reshape.264 = bf16[1536,576]{1,0:T(8,128)(2,1)S(1)} reshape(bf16[576,1536]{1,0:T(8,128)(2,1)} %get-tuple-element.128) | data formatting | bytes 3538944 | tf_op jit(solution)/shard_map/reshape | solution.py:299
  134.9 8.2 %attend.2 = (bf16[9,64,256]{2,1,0:T(8,128)(2,1)S(1)}, f32[9,1,256]{2,1,0:T(1,128)S(1)}) custom-call(bf16[9,64,256]{2,1,0:T(8,128)(2,1)S(1)} %maximum_multiply_fusion.q_ref, bf16[6,64,1024]{2,1,0:T(8,128)(2,1)S(1)} %pad_maximum_fusion.2.k_ref.v_ref, bf16[6,64,1024]{2,1,0:T(8,128)(2,1)S(1)} %pad_maximum_fusion.2.k_ref.v_ref, s32[1,256]{1,0:T(1,128)S(1)} %bitcast.144, ...), custom_call_target="tpu_custom_call" | custom-call | flops 603979776 | bytes 2097152 | tf_op jit(solution)/shard_map/attend/pallas_call | solution.py:111
  147.9 4.1 multiply_convert_fusion.5
  153.0 3.6 broadcast_select_fusion.4
  162.0 4.4 %reshape.266 = bf16[1536,576]{1,0:T(8,128)(2,1)S(1)} reshape(bf16[576,1536]{1,0:T(8,128)(2,1)} %get-tuple-element.126) | data formatting | bytes 3538944 | tf_op jit(solution)/shard_map/reshape | solution.py:299
  172.0 8.4 %attend.3 = (bf16[9,64,256]{2,1,0:T(8,128)(2,1)S(1)}, f32[9,1,256]{2,1,0:T(1,128)S(1)}) custom-call(bf16[9,64,256]{2,1,0:T(8,128)(2,1)S(1)} %maximum_multiply_fusion.1.q_ref, bf16[6,64,1024]{2,1,0:T(8,128)(2,1)S(1)} %pad_maximum_fusion.3.k_ref.v_ref, bf16[6,64,1024]{2,1,0:T(8,128)(2,1)S(1)} %pad_maximum_fusion.3.k_ref.v_ref, s32[1,256]{1,0:T(1,128)S(1)} %bitcast.145, ...), custom_call_target="tpu_custom_call" | custom-call | flops 603979776 | bytes 2097152 | tf_op jit(solution)/shard_map/attend/pallas_call | solution.py:111
  183.8 3.0 multiply_convert_fusion.3
  199.8 11.4 %attend_back.2 = (f32[9,64,256]{2,1,0:T(8,128)S(1)}, f32[3,64,1024]{2,1,0:T(8,128)S(1)}, f32[3,64,1024]{2,1,0:T(8,128)S(1)}) custom-call(bf16[9,64,256]{2,1,0:T(8,128)(2,1)S(1)} %maximum_multiply_fusion.1.q_ref, bf16[6,64,1024]{2,1,0:T(8,128)(2,1)S(1)} %pad_maximum_fusion.3.k_ref.v_ref, bf16[6,64,1024]{2,1,0:T(8,128)(2,1)S(1)} %pad_maximum_fusion.3.k_ref.v_ref, ...), custom_call_target="tpu_custom_call" | custom-call | flops 1509949440 | bytes 4194304 | tf_op jit(solution)/shard_map/attend_back/pallas_call | solution.py:133
  211.2 3.9 copy.51
  215.1 5.3 %reshape.269 = bf16[576,1536]{1,0:T(8,128)(2,1)} reshape(bf16[1536,576]{1,0:T(8,128)(2,1)} %copy.51) | data formatting | bytes 3538944 | tf_op jit(solution)/shard_map/reshape | solution.py:337
  236.9 3.7 collective-permute-done.31
  255.6 4.2 reshape.270
  271.8 3.7 collective-permute-start.40
  280.9 11.7 %attend_back.3 = (f32[9,64,256]{2,1,0:T(8,128)S(1)}, f32[3,64,1024]{2,1,0:T(8,128)S(1)}, f32[3,64,1024]{2,1,0:T(8,128)S(1)}) custom-call(bf16[9,64,256]{2,1,0:T(8,128)(2,1)S(1)} %copy-done.6, bf16[6,64,1024]{2,1,0:T(8,128)(2,1)S(1)} %pad_maximum_fusion.2.k_ref.v_ref, bf16[6,64,1024]{2,1,0:T(8,128)(2,1)S(1)} %pad_maximum_fusion.2.k_ref.v_ref, ...), custom_call_target="tpu_custom_call" | custom-call | flops 1509949440 | bytes 4194304 | tf_op jit(solution)/shard_map/attend_back/pallas_call | solution.py:133
  300.3 4.5 %collective-permute-done.48 = bf16[144,384]{1,0:T(8,128)(2,1)S(1)} collective-permute-done((bf16[144,384]{1,0:T(8,128)(2,1)S(1)}, bf16[144,384]{1,0:T(8,128)(2,1)S(1)}, u32[]{:S(2)}, u32[]{:S(2)}) %collective-permute-start.48) | collective-permute-done | bytes 110624 | tf_op jit(solution)/shard_map/ppermute | solution.py:26
  331.4 7.6 %collective-permute-done.44 = bf16[144,1536]{1,0:T(8,128)(2,1)S(1)} collective-permute-done((bf16[144,1536]{1,0:T(8,128)(2,1)}, bf16[144,1536]{1,0:T(8,128)(2,1)S(1)}, u32[]{:S(2)}, u32[]{:S(2)}) %collective-permute-start.44) | collective-permute-done | bytes 442400 | tf_op jit(solution)/shard_map/ppermute | solution.py:26
  339.4 9.7 %collective-permute-done.70 = bf16[144,1536]{1,0:T(8,128)(2,1)S(1)} collective-permute-done((bf16[144,1536]{1,0:T(8,128)(2,1)S(1)}, bf16[144,1536]{1,0:T(8,128)(2,1)S(1)}, u32[]{:S(2)}, u32[]{:S(2)}) %collective-permute-start.70) | collective-permute-done | bytes 442400 | tf_op jit(solution)/shard_map/ppermute | solution.py:26
  358.3 4.2 collective-permute-done.62
  365.9 5.2 %collective-permute-done.72 = bf16[144,384]{1,0:T(8,128)(2,1)S(1)} collective-permute-done((bf16[144,384]{1,0:T(8,128)(2,1)S(1)}, bf16[144,384]{1,0:T(8,128)(2,1)S(1)}, u32[]{:S(2)}, u32[]{:S(2)}) %collective-permute-start.72) | collective-permute-done | bytes 110624 | tf_op jit(solution)/shard_map/ppermute | solution.py:26
  374.7 5.5 %collective-permute-done.65 = bf16[144,384]{1,0:T(8,128)(2,1)S(1)} collective-permute-done((bf16[144,384]{1,0:T(8,128)(2,1)S(1)}, bf16[144,384]{1,0:T(8,128)(2,1)S(1)}, u32[]{:S(2)}, u32[]{:S(2)}) %collective-permute-start.65) | collective-permute-done | bytes 110624 | tf_op jit(solution)/shard_map/ppermute | solution.py:26
  388.3 3.5 collective-permute-done.54
  391.9 4.6 %collective-permute-done.53 = bf16[144,1536]{1,0:T(8,128)(2,1)S(1)} collective-permute-done((bf16[144,1536]{1,0:T(8,128)(2,1)S(1)}, bf16[144,1536]{1,0:T(8,128)(2,1)S(1)}, u32[]{:S(2)}, u32[]{:S(2)}) %collective-permute-start.53) | collective-permute-done | bytes 442400 | tf_op jit(solution)/shard_map/ppermute | solution.py:26
  413.3 5.5 %collective-permute-done.59 = bf16[144,384]{1,0:T(8,128)(2,1)S(1)} collective-permute-done((bf16[144,384]{1,0:T(8,128)(2,1)S(1)}, bf16[144,384]{1,0:T(8,128)(2,1)S(1)}, u32[]{:S(2)}, u32[]{:S(2)}) %collective-permute-start.59) | collective-permute-done | bytes 110624 | tf_op jit(solution)/shard_map/ppermute | solution.py:26
  (472 shorter events, 216.6 us)
Async XLA Ops:
  5.7 52.2 %collective-permute-start.6 = (bf16[2,144]{1,0:T(2,128)(2,1)S(1)}, bf16[2,144]{1,0:T(2,128)(2,1)S(1)}, u32[]{:S(2)}, u32[]{:S(2)}) collective-permute-start(bf16[2,144]{1,0:T(2,128)(2,1)S(1)} %pad_maximum_fusion.13), channel_id=1, source_target_pairs={{0,16},{16,0},{1,17},{17,1},{2,18},{18,2},{3,19},{19,3},{4,20},{20... | collective-permute-start | bytes 1736 | tf_op jit(solution)/shard_map/ppermute | solution.py:26
  11.7 21.7 %collective-permute-start.3 = (bf16[144,1536]{1,0:T(8,128)(2,1)S(1)}, bf16[144,1536]{1,0:T(8,128)(2,1)S(1)}, u32[]{:S(2)}, u32[]{:S(2)}) collective-permute-start(bf16[144,1536]{1,0:T(8,128)(2,1)S(1)} %get-tuple-element.125), channel_id=1, source_target_pairs={{0,2},{1,3},{2,0},{3,1},{4,6},{5,7},{6,4},{7,5},{8,10},{9,11},{10,... | collective-permute-start | bytes 1327112 | tf_op jit(solution)/shard_map/ppermute | solution.py:26
  13.2 20.2 %collective-permute-start.4 = (bf16[144,1536]{1,0:T(8,128)(2,1)S(1)}, bf16[144,1536]{1,0:T(8,128)(2,1)S(1)}, u32[]{:S(2)}, u32[]{:S(2)}) collective-permute-start(bf16[144,1536]{1,0:T(8,128)(2,1)S(1)} %get-tuple-element.125), channel_id=1, source_target_pairs={{0,3},{1,2},{2,1},{3,0},{4,7},{5,6},{6,5},{7,4},{8,11},{9,10},{10,... | collective-permute-start | bytes 1327112 | tf_op jit(solution)/shard_map/ppermute | solution.py:26
  34.7 20.9 %collective-permute-start.14 = (bf16[144,1536]{1,0:T(8,128)(2,1)S(1)}, bf16[144,1536]{1,0:T(8,128)(2,1)S(1)}, u32[]{:S(2)}, u32[]{:S(2)}) collective-permute-start(bf16[144,1536]{1,0:T(8,128)(2,1)S(1)} %get-tuple-element.44), channel_id=1, source_target_pairs={{0,2},{1,3},{2,0},{3,1},{4,6},{5,7},{6,4},{7,5},{8,10},{9,11},{10,... | collective-permute-start | bytes 1327112 | tf_op jit(solution)/shard_map/ppermute | solution.py:26
  35.6 20.9 %collective-permute-start.15 = (bf16[144,1536]{1,0:T(8,128)(2,1)S(1)}, bf16[144,1536]{1,0:T(8,128)(2,1)S(1)}, u32[]{:S(2)}, u32[]{:S(2)}) collective-permute-start(bf16[144,1536]{1,0:T(8,128)(2,1)S(1)} %get-tuple-element.44), channel_id=1, source_target_pairs={{0,3},{1,2},{2,1},{3,0},{4,7},{5,6},{6,5},{7,4},{8,11},{9,10},{10,... | collective-permute-start | bytes 1327112 | tf_op jit(solution)/shard_map/ppermute | solution.py:26
  57.2 15.1 %collective-permute-start.17 = (bf16[144,1536]{1,0:T(8,128)(2,1)S(1)}, bf16[144,1536]{1,0:T(8,128)(2,1)}, u32[]{:S(2)}, u32[]{:S(2)}) collective-permute-start(bf16[144,1536]{1,0:T(8,128)(2,1)S(1)} %get-tuple-element.46), channel_id=1, source_target_pairs={{0,1},{1,0},{2,3},{3,2},{4,5},{5,4},{6,7},{7,6},{8,9},{9,8},{10,11... | collective-permute-start | bytes 1327112 | tf_op jit(solution)/shard_map/ppermute | solution.py:26
  67.0 49.2 %collective-permute-start.5 = (bf16[576,1536]{1,0:T(8,128)(2,1)S(1)}, bf16[576,1536]{1,0:T(8,128)(2,1)}, u32[]{:S(2)}, u32[]{:S(2)}) collective-permute-start(bf16[576,1536]{1,0:T(8,128)(2,1)S(1)} %constant_dynamic-update-slice_fusion.28), channel_id=1, source_target_pairs={{0,16},{16,0},{1,17},{17,1},{2,18},{18,2},{3,19},{19,3},{4,20},{20... | collective-permute-start | bytes 5308424 | tf_op jit(solution)/shard_map/ppermute | solution.py:26
  67.1 22.1 %collective-permute-start.18 = (bf16[144,1536]{1,0:T(8,128)(2,1)S(1)}, bf16[144,1536]{1,0:T(8,128)(2,1)S(1)}, u32[]{:S(2)}, u32[]{:S(2)}) collective-permute-start(bf16[144,1536]{1,0:T(8,128)(2,1)S(1)} %get-tuple-element.46), channel_id=1, source_target_pairs={{0,2},{1,3},{2,0},{3,1},{4,6},{5,7},{6,4},{7,5},{8,10},{9,11},{10,... | collective-permute-start | bytes 1327112 | tf_op jit(solution)/shard_map/ppermute | solution.py:26
  68.4 21.5 %collective-permute-start.19 = (bf16[144,1536]{1,0:T(8,128)(2,1)S(1)}, bf16[144,1536]{1,0:T(8,128)(2,1)S(1)}, u32[]{:S(2)}, u32[]{:S(2)}) collective-permute-start(bf16[144,1536]{1,0:T(8,128)(2,1)S(1)} %get-tuple-element.46), channel_id=1, source_target_pairs={{0,3},{1,2},{2,1},{3,0},{4,7},{5,6},{6,5},{7,4},{8,11},{9,10},{10,... | collective-permute-start | bytes 1327112 | tf_op jit(solution)/shard_map/ppermute | solution.py:26
  92.4 53.0 %collective-permute-start.16 = (bf16[576,1536]{1,0:T(8,128)(2,1)}, bf16[576,1536]{1,0:T(8,128)(2,1)}, u32[]{:S(2)}, u32[]{:S(2)}) collective-permute-start(bf16[576,1536]{1,0:T(8,128)(2,1)} %constant_dynamic-update-slice_fusion.24), channel_id=1, source_target_pairs={{0,16},{16,0},{1,17},{17,1},{2,18},{18,2},{3,19},{19,3},{4,20},{20... | collective-permute-start | bytes 5308424 | tf_op jit(solution)/shard_map/ppermute | solution.py:26
  92.5 22.1 %collective-permute-start.25 = (bf16[144,1536]{1,0:T(8,128)(2,1)S(1)}, bf16[144,1536]{1,0:T(8,128)(2,1)S(1)}, u32[]{:S(2)}, u32[]{:S(2)}) collective-permute-start(bf16[144,1536]{1,0:T(8,128)(2,1)S(1)} %get-tuple-element.49), channel_id=1, source_target_pairs={{0,2},{1,3},{2,0},{3,1},{4,6},{5,7},{6,4},{7,5},{8,10},{9,11},{10,... | collective-permute-start | bytes 1327112 | tf_op jit(solution)/shard_map/ppermute | solution.py:26
  93.4 22.0 %collective-permute-start.26 = (bf16[144,1536]{1,0:T(8,128)(2,1)S(1)}, bf16[144,1536]{1,0:T(8,128)(2,1)S(1)}, u32[]{:S(2)}, u32[]{:S(2)}) collective-permute-start(bf16[144,1536]{1,0:T(8,128)(2,1)S(1)} %get-tuple-element.49), channel_id=1, source_target_pairs={{0,3},{1,2},{2,1},{3,0},{4,7},{5,6},{6,5},{7,4},{8,11},{9,10},{10,... | collective-permute-start | bytes 1327112 | tf_op jit(solution)/shard_map/ppermute | solution.py:26
  103.8 49.2 %collective-permute-start.20 = (bf16[576,1536]{1,0:T(8,128)(2,1)}, bf16[576,1536]{1,0:T(8,128)(2,1)}, u32[]{:S(2)}, u32[]{:S(2)}) collective-permute-start(bf16[576,1536]{1,0:T(8,128)(2,1)} %constant_dynamic-update-slice_fusion.20), channel_id=1, source_target_pairs={{0,16},{16,0},{1,17},{17,1},{2,18},{18,2},{3,19},{19,3},{4,20},{20... | collective-permute-start | bytes 5308424 | tf_op jit(solution)/shard_map/ppermute | solution.py:26
  130.1 51.4 %collective-permute-start.27 = (bf16[576,1536]{1,0:T(8,128)(2,1)}, bf16[576,1536]{1,0:T(8,128)(2,1)}, u32[]{:S(2)}, u32[]{:S(2)}) collective-permute-start(bf16[576,1536]{1,0:T(8,128)(2,1)} %constant_dynamic-update-slice_fusion.16), channel_id=1, source_target_pairs={{0,16},{16,0},{1,17},{17,1},{2,18},{18,2},{3,19},{19,3},{4,20},{20... | collective-permute-start | bytes 5308424 | tf_op jit(solution)/shard_map/ppermute | solution.py:26
  188.5 34.4 %collective-permute-start.28 = (bf16[256,576]{0,1:T(8,128)(2,1)}, bf16[256,576]{0,1:T(8,128)(2,1)}, u32[]{:S(2)}, u32[]{:S(2)}) collective-permute-start(bf16[256,576]{0,1:T(8,128)(2,1)} %get-tuple-element.210), channel_id=1, source_target_pairs={{0,16},{16,0},{1,17},{17,1},{2,18},{18,2},{3,19},{19,3},{4,20},{20... | collective-permute-start | bytes 884744 | tf_op jit(solution)/shard_map/ppermute | solution.py:26
  191.7 33.4 %collective-permute-start.29 = (bf16[576,1536]{1,0:T(8,128)(2,1)}, bf16[576,1536]{1,0:T(8,128)(2,1)}, u32[]{:S(2)}, u32[]{:S(2)}) collective-permute-start(bf16[576,1536]{1,0:T(8,128)(2,1)} %get-tuple-element.213), channel_id=1, source_target_pairs={{0,16},{16,0},{1,17},{17,1},{2,18},{18,2},{3,19},{19,3},{4,20},{20... | collective-permute-start | bytes 5308424 | tf_op jit(solution)/shard_map/ppermute | solution.py:26
  232.2 34.8 %collective-permute-start.35 = (bf16[144,1536]{1,0:T(8,128)(2,1)}, bf16[144,1536]{1,0:T(8,128)(2,1)}, u32[]{:S(2)}, u32[]{:S(2)}) collective-permute-start(bf16[144,1536]{1,0:T(8,128)(2,1)} %get-tuple-element.145), channel_id=1, source_target_pairs={{0,3},{1,2},{2,1},{3,0},{4,7},{5,6},{6,5},{7,4},{8,11},{9,10},{10,... | collective-permute-start | bytes 1327112 | tf_op jit(solution)/shard_map/ppermute | solution.py:26
  233.5 33.6 %collective-permute-start.34 = (bf16[144,1536]{1,0:T(8,128)(2,1)}, bf16[144,1536]{1,0:T(8,128)(2,1)}, u32[]{:S(2)}, u32[]{:S(2)}) collective-permute-start(bf16[144,1536]{1,0:T(8,128)(2,1)} %get-tuple-element.146), channel_id=1, source_target_pairs={{0,2},{1,3},{2,0},{3,1},{4,6},{5,7},{6,4},{7,5},{8,10},{9,11},{10,... | collective-permute-start | bytes 1327112 | tf_op jit(solution)/shard_map/ppermute | solution.py:26
  236.3 30.7 %collective-permute-start.33 = (bf16[144,1536]{1,0:T(8,128)(2,1)}, bf16[144,1536]{1,0:T(8,128)(2,1)}, u32[]{:S(2)}, u32[]{:S(2)}) collective-permute-start(bf16[144,1536]{1,0:T(8,128)(2,1)} %get-tuple-element.144), channel_id=1, source_target_pairs={{0,1},{1,0},{2,3},{3,2},{4,5},{5,4},{6,7},{7,6},{8,9},{9,8},{10,11... | collective-permute-start | bytes 1327112 | tf_op jit(solution)/shard_map/ppermute | solution.py:26
  249.7 19.3 %collective-permute-start.36 = (bf16[576,1536]{1,0:T(8,128)(2,1)}, bf16[576,1536]{1,0:T(8,128)(2,1)}, u32[]{:S(2)}, u32[]{:S(2)}) collective-permute-start(bf16[576,1536]{1,0:T(8,128)(2,1)} %broadcast_select_fusion.2), channel_id=1, source_target_pairs={{0,16},{16,0},{1,17},{17,1},{2,18},{18,2},{3,19},{19,3},{4,20},{20... | collective-permute-start | bytes 5308424 | tf_op jit(solution)/shard_map/ppermute | solution.py:26
  252.8 25.7 %collective-permute-start.37 = (bf16[576,1536]{1,0:T(8,128)(2,1)}, bf16[576,1536]{1,0:T(8,128)(2,1)}, u32[]{:S(2)}, u32[]{:S(2)}) collective-permute-start(bf16[576,1536]{1,0:T(8,128)(2,1)} %get-tuple-element.217), channel_id=1, source_target_pairs={{0,16},{16,0},{1,17},{17,1},{2,18},{18,2},{3,19},{19,3},{4,20},{20... | collective-permute-start | bytes 5308424 | tf_op jit(solution)/shard_map/ppermute | solution.py:26
  271.8 20.9 %collective-permute-start.40 = (bf16[144,384]{1,0:T(8,128)(2,1)S(1)}, bf16[144,384]{1,0:T(8,128)(2,1)S(1)}, u32[]{:S(2)}, u32[]{:S(2)}) collective-permute-start(bf16[144,384]{1,0:T(8,128)(2,1)S(1)} %get-tuple-element.179), channel_id=1, source_target_pairs={{0,12},{4,8},{8,4},{12,0},{1,13},{5,9},{9,5},{13,1},{2,14},{6,10},... | collective-permute-start | bytes 331784 | tf_op jit(solution)/shard_map/ppermute | solution.py:26
  275.4 17.2 %collective-permute-start.39 = (bf16[144,384]{1,0:T(8,128)(2,1)S(1)}, bf16[144,384]{1,0:T(8,128)(2,1)S(1)}, u32[]{:S(2)}, u32[]{:S(2)}) collective-permute-start(bf16[144,384]{1,0:T(8,128)(2,1)S(1)} %get-tuple-element.180), channel_id=1, source_target_pairs={{0,8},{4,12},{8,0},{12,4},{1,9},{5,13},{9,1},{13,5},{2,10},{6,14},... | collective-permute-start | bytes 331784 | tf_op jit(solution)/shard_map/ppermute | solution.py:26
  275.4 17.2 %collective-permute-start.38 = (bf16[144,384]{1,0:T(8,128)(2,1)S(1)}, bf16[144,384]{1,0:T(8,128)(2,1)S(1)}, u32[]{:S(2)}, u32[]{:S(2)}) collective-permute-start(bf16[144,384]{1,0:T(8,128)(2,1)S(1)} %get-tuple-element.178), channel_id=1, source_target_pairs={{0,4},{4,0},{8,12},{12,8},{1,5},{5,1},{9,13},{13,9},{2,6},{6,2},{1... | collective-permute-start | bytes 331784 | tf_op jit(solution)/shard_map/ppermute | solution.py:26
  277.3 52.9 %collective-permute-start.46 = (bf16[144,1536]{1,0:T(8,128)(2,1)}, bf16[144,1536]{1,0:T(8,128)(2,1)S(1)}, u32[]{:S(2)}, u32[]{:S(2)}) collective-permute-start(bf16[144,1536]{1,0:T(8,128)(2,1)} %get-tuple-element.142), channel_id=1, source_target_pairs={{0,3},{1,2},{2,1},{3,0},{4,7},{5,6},{6,5},{7,4},{8,11},{9,10},{10,... | collective-permute-start | bytes 1327112 | tf_op jit(solution)/shard_map/ppermute | solution.py:26
  305.9 25.5 %collective-permute-start.45 = (bf16[144,1536]{1,0:T(8,128)(2,1)}, bf16[144,1536]{1,0:T(8,128)(2,1)S(1)}, u32[]{:S(2)}, u32[]{:S(2)}) collective-permute-start(bf16[144,1536]{1,0:T(8,128)(2,1)} %get-tuple-element.143), channel_id=1, source_target_pairs={{0,2},{1,3},{2,0},{3,1},{4,6},{5,7},{6,4},{7,5},{8,10},{9,11},{10,... | collective-permute-start | bytes 1327112 | tf_op jit(solution)/shard_map/ppermute | solution.py:26
  327.3 21.8 %collective-permute-start.70 = (bf16[144,1536]{1,0:T(8,128)(2,1)S(1)}, bf16[144,1536]{1,0:T(8,128)(2,1)S(1)}, u32[]{:S(2)}, u32[]{:S(2)}) collective-permute-start(bf16[144,1536]{1,0:T(8,128)(2,1)S(1)} %get-tuple-element.136), channel_id=1, source_target_pairs={{0,3},{1,2},{2,1},{3,0},{4,7},{5,6},{6,5},{7,4},{8,11},{9,10},{10,... | collective-permute-start | bytes 1327112 | tf_op jit(solution)/shard_map/ppermute | solution.py:26
  328.5 23.1 %collective-permute-start.69 = (bf16[144,1536]{1,0:T(8,128)(2,1)S(1)}, bf16[144,1536]{1,0:T(8,128)(2,1)S(1)}, u32[]{:S(2)}, u32[]{:S(2)}) collective-permute-start(bf16[144,1536]{1,0:T(8,128)(2,1)S(1)} %get-tuple-element.137), channel_id=1, source_target_pairs={{0,2},{1,3},{2,0},{3,1},{4,6},{5,7},{6,4},{7,5},{8,10},{9,11},{10,... | collective-permute-start | bytes 1327112 | tf_op jit(solution)/shard_map/ppermute | solution.py:26
  330.2 24.0 %collective-permute-start.68 = (bf16[144,1536]{1,0:T(8,128)(2,1)S(1)}, bf16[144,1536]{1,0:T(8,128)(2,1)S(1)}, u32[]{:S(2)}, u32[]{:S(2)}) collective-permute-start(bf16[144,1536]{1,0:T(8,128)(2,1)S(1)} %get-tuple-element.135), channel_id=1, source_target_pairs={{0,1},{1,0},{2,3},{3,2},{4,5},{5,4},{6,7},{7,6},{8,9},{9,8},{10,11... | collective-permute-start | bytes 1327112 | tf_op jit(solution)/shard_map/ppermute | solution.py:26
  331.3 49.0 %collective-permute-start.51 = (bf16[576,1536]{1,0:T(8,128)(2,1)S(1)}, bf16[576,1536]{1,0:T(8,128)(2,1)S(1)}, u32[]{:S(2)}, u32[]{:S(2)}) collective-permute-start(bf16[576,1536]{1,0:T(8,128)(2,1)S(1)} %broadcast_select_fusion), channel_id=1, source_target_pairs={{0,16},{16,0},{1,17},{17,1},{2,18},{18,2},{3,19},{19,3},{4,20},{20... | collective-permute-start | bytes 5308424 | tf_op jit(solution)/shard_map/ppermute | solution.py:26
  339.3 42.8 %collective-permute-start.50 = (bf16[256,576]{0,1:T(8,128)(2,1)S(1)}, bf16[256,576]{0,1:T(8,128)(2,1)S(1)}, u32[]{:S(2)}, u32[]{:S(2)}) collective-permute-start(bf16[256,576]{0,1:T(8,128)(2,1)S(1)} %convert_select_fusion.2), channel_id=1, source_target_pairs={{0,16},{16,0},{1,17},{17,1},{2,18},{18,2},{3,19},{19,3},{4,20},{20... | collective-permute-start | bytes 884744 | tf_op jit(solution)/shard_map/ppermute | solution.py:26
  386.2 15.0 %collective-permute-start.76 = (bf16[144,384]{1,0:T(8,128)(2,1)S(1)}, bf16[144,384]{1,0:T(8,128)(2,1)S(1)}, u32[]{:S(2)}, u32[]{:S(2)}) collective-permute-start(bf16[144,384]{1,0:T(8,128)(2,1)S(1)} %get-tuple-element.119), channel_id=1, source_target_pairs={{0,12},{4,8},{8,4},{12,0},{1,13},{5,9},{9,5},{13,1},{2,14},{6,10},... | collective-permute-start | bytes 331784 | tf_op jit(solution)/shard_map/ppermute | solution.py:26
  (119 other events, 737.7 us)

commit v3 on v2

--- a/solution.py
+++ b/solution.py
@@ -156,8 +156,8 @@
     )(queries, keys_values, keys_values, *marks, lse, grad_out)
 
 
-def layer_forward(activation, weights, gains, cos, sin, marks):
-    qkv_weight, output_weight, gate_up, down_weight = weights
+def layer_forward(activation, weights, gains, cos, sin, marks, at_keys, at_attended):
+    qkv_weight, output_weight, down_weight = weights
     rows = activation.shape[0]
     fsdp = lax.axis_size("fsdp")
     normed = norm_rows(activation, gains[0]).astype(BF16)
@@ -169,15 +169,17 @@
     keys_values = jnp.concatenate(
         [mine] + [exchange(mine, "fsdp", d) for d in range(1, fsdp)], 2
     )
+    keys_values = at_keys(keys_values)
     attended, lse = attend(queries, keys_values, marks)
-    attended = attended.reshape(QD, rows)
+    attended, gate_up = at_attended(attended.reshape(QD, rows))
     middle = activation + dot(attended, output_weight, (0, 0))
     normed_mid = norm_rows(middle, gains[1]).astype(BF16)
     gate, lift = [dot(normed_mid, weight, (1, 0)) for weight in gate_up]
     hidden = (gate * jax.nn.sigmoid(gate) * lift).astype(BF16)
     result = middle + dot(hidden, down_weight, (1, 0))
+    weights = (qkv_weight, output_weight, gate_up, down_weight)
     kept = (activation, normed, queries, keys_values, lse, attended, middle, normed_mid, gate, lift, hidden)
-    return result, kept
+    return result, kept, weights
 
 
 def feedforward_back(grad, kept, weights, gains):
@@ -228,16 +230,23 @@
     return own.astype(BF16)
 
 
-def collect(share, axis, dim):
-    size, me = lax.axis_size(axis), lax.axis_index(axis)
-    span = share.shape[dim]
-    shape = list(share.shape)
-    shape[dim] = span * size
-    full = jnp.zeros(shape, share.dtype)
-    for d in range(size):
-        block = share if d == 0 else exchange(share, axis, d)
+def fetch(share, axis):
+    return [share] + [exchange(share, axis, d) for d in range(1, lax.axis_size(axis))]
+
+
+def place(blocks, axis, dim):
+    me = lax.axis_index(axis)
+    span = blocks[0].shape[dim]
+    shape = list(blocks[0].shape)
+    shape[dim] = span * len(blocks)
+    full = jnp.zeros(shape, blocks[0].dtype)
+    for d, block in enumerate(blocks):
         full = lax.dynamic_update_slice_in_dim(full, block, (me ^ d) * span, dim)
     return full
+
+
+def collect(share, axis, dim):
+    return place(fetch(share, axis), axis, dim)
 
 
 def tie(*arrays):
@@ -274,30 +283,27 @@
         other = exchange(full, "section", 1)
         return jnp.where(on_first, full, other), jnp.where(on_first, other, full)
 
-    weights = []
-    before = None
-    for layer in range(2):
-        pairs = []
-        for kind in range(2):
-            share = shares[kind][layer]
-            if before is not None:
-                share, before = tie(share, before)
-                if kind == 1:
-                    pairs[0] = before
-                elif layer == 1:
-                    weights[0][1] = before
-            before = collect(share, "fsdp", 0)
-            pairs.append(before)
-        weights.append(pairs)
-    for layer in range(2):
-        attention, down_full = both_parts(weights[layer][0])
-        gate_full, up_full = both_parts(weights[layer][1])
-        weights[layer] = (
-            attention[:, :qkv],
-            attention[:, qkv:],
-            (gate_full, up_full),
-            down_full.reshape(-1, width),
-        )
+    def attention_part(blocks):
+        attention, down_full = both_parts(place(blocks, "fsdp", 0))
+        return attention[:, :qkv], attention[:, qkv:], down_full.reshape(-1, width)
+
+    pending = {"attention0": fetch(shares[0][0], "fsdp")}
+    share, *blocks = tie(shares[1][0], *pending["attention0"])
+    pending["feed0"] = fetch(share, "fsdp")
+
+    def keys_here(keys_values):
+        keys_values, share = tie(keys_values, shares[0][1])
+        pending["attention1"] = fetch(share, "fsdp")
+        return keys_values
+
+    def attended_here(layer):
+        def hook(attended):
+            attended, share, *arrived = tie(attended, shares[1][1], *pending["feed%d" % layer])
+            if layer == 0:
+                pending["feed1"] = fetch(share, "fsdp")
+            return attended, both_parts(place(arrived, "fsdp", 0))
+
+        return hook
 
     segment_ids = lax.dynamic_index_in_dim(segments[:, 0], section, 0, keepdims=False)
     activation = lax.dynamic_index_in_dim(inputs[:, 0], section, 0, keepdims=False).astype(F32)
@@ -312,9 +318,21 @@
     angle = freqs[:, None] * (pos - start).astype(F32)[None, :]
     cos, sin = jnp.cos(angle), jnp.sin(angle)
 
-    result, kept0 = layer_forward(activation, weights[0], gains[0], cos, sin, marks)
-    handed = result.astype(BF16)
-    result, kept1 = layer_forward(handed.astype(F32), weights[1], gains[1], cos, sin, marks)
+    result, kept0, weights0 = layer_forward(
+        activation, attention_part(blocks), gains[0], cos, sin, marks, keys_here, attended_here(0)
+    )
+    handed, *blocks = tie(result.astype(BF16), *pending["attention1"])
+    result, kept1, weights1 = layer_forward(
+        handed.astype(F32),
+        attention_part(blocks),
+        gains[1],
+        cos,
+        sin,
+        marks,
+        lambda keys_values: keys_values,
+        attended_here(1),
+    )
+    weights = (weights0, weights1)
     final = result.astype(BF16)
 
     def sorted_out(first, second, send_first, send_second):
@@ -356,32 +374,31 @@
         returned.astype(F32), kept0, weights[0], gains[0]
     )
     heads, output_grad = heads_back(middle_grad, kept0, 0)
-    heads, early1, late1 = tie(heads, early1, late1)
+    early0 = sum_section(gate_grad, up_grad, on_first)
+    heads, early1, late1, early0 = tie(heads, early1, late1, early0)
     early1 = sum_scatter(early1, "rep", 1)
     late1 = sum_scatter(late1, "fsdp", 0)
-    early0 = sum_section(gate_grad, up_grad, on_first)
     dq, dk, dv = attend_back(kept0[2], kept0[3], marks, kept0[4], heads)
-    dq, dk, dv, early0, early1 = tie(dq, dk, dv, early0, early1)
+    dq, dk, dv, early1 = tie(dq, dk, dv, early1)
+    early0 = sum_scatter(early0, "fsdp", 0)
     early1 = collect(early1, "rep", 1)
     grad, qkv_grad, attention_gain0 = projections_back(
         middle_grad, dq, dk, dv, kept0, weights[0], gains[0], cos, sin
     )
-    grad, late1, early1 = tie(grad, late1, early1)
-    early0 = sum_scatter(early0, "fsdp", 0)
+    grad, late1, early1, early0 = tie(grad, late1, early1, early0)
     late0 = second_chunk(qkv_grad, output_grad, down_grad)
     input_grad = sorted_out(grad, returned.astype(F32), grad.astype(BF16), returned)
-
-    def gathered(part):
-        return collect(sum_scatter(part, "rep", 1), "rep", 1)
 
     def owned(part0, part1):
         other = exchange(jnp.where(on_first, part1, part0), "section", 1)
         left = jnp.where(on_first, part0, other).astype(F32)
         return left, jnp.where(on_first, other, part1).astype(F32)
 
-    late1 = gathered(late1)
-    early0 = gathered(early0)
-    late0 = gathered(sum_scatter(late0, "fsdp", 0))
+    late1, early0, late0 = tie(late1, early0, late0)
+    late1, early0 = sum_scatter(late1, "rep", 1), sum_scatter(early0, "rep", 1)
+    late1, early0, late0 = tie(late1, early0, sum_scatter(late0, "fsdp", 0))
+    late1, early0 = collect(late1, "rep", 1), collect(early0, "rep", 1)
+    late0 = collect(sum_scatter(late0, "rep", 1), "rep", 1)
     gate_sum, up_sum = owned(early0, early1)
     rest, down_sum = owned(late0, late1)
 

time: 431 us -> 435 us (level)
  waiting for transfers between devices: 155 us -> 164 us
  other arithmetic: 37.3 us -> 31 us
  starting transfers between devices: 85.8 us -> 90.3 us
    ppermute x85, waiting for transfers between devices: 155 us -> 164 us  [exchange(): return lax.ppermute(block, axis, [(i, i ^ distance) for i in range(size)])]
    ppermute x85, starting transfers between devices: 85.8 us -> 90.3 us  [exchange(): return lax.ppermute(block, axis, [(i, i ^ distance) for i in range(size)])]
    dynamic_update_slice x32 -> x35, local copies, waits for them, and re-layouts: 11.2 us -> 8.2 us  [place(): full = lax.dynamic_update_slice_in_dim(full, block, (me ^ d) * span, dim)]
    unnamed x132 -> x146, local copies, waits for them, and re-layouts: 10.1 us -> 10.1 us
  transfers between devices with their start and end apart: 85 -> 85, of which waited for: 38 -> 35; matrix products, arithmetic and copies ran while one was open for 28% -> 21% of each run, Pallas kernels for 9% -> 9%
where the time goes in v3:
time: 435 us; the launch traced here: 430 us
  waiting for transfers between devices  164 us (38%)
  starting transfers between devices  90.3 us (21%)
  local copies, waits for them, and re-layouts  55.7 us (13%)
  matrix products  46.7 us (11%)
  Pallas kernels  39.9 us (9%)
  other arithmetic  31 us (7%)
    ppermute x85, waiting for transfers between devices, exchange(): return lax.ppermute(block, axis, [(i, i ^ distance) for i in range(size)])  164 us
    ppermute x85, starting transfers between devices, exchange(): return lax.ppermute(block, axis, [(i, i ^ distance) for i in range(size)])  90.3 us
    dot_general x30, matrix products, dot(): lax.dot_general(left, right, ((dims[:1], dims[1:]), ((), ())), preferred_...  46.7 us
    pallas_call x2, Pallas kernels, attend_back(): pl.pallas_call(attend_back_kernel, grid=(QH,), in_specs=attention_specs(q...  23.1 us
    pallas_call x2, Pallas kernels, attend(): pl.pallas_call(attend_kernel, grid=(QH,), in_specs=attention_specs(querie...  16.8 us
    reshape x2, local copies, waits for them, and re-layouts, attention_part(): down_full.reshape(-1, width)  10.8 us
    unnamed x146, local copies, waits for them, and re-layouts  10.1 us
    reshape x2, local copies, waits for them, and re-layouts, second_chunk(): down_grad.reshape(qkv_grad.shape[0], half)  9.52 us
  transfers between devices with their start and end apart: 85, of which 35 were waited for; matrix products, arithmetic and copies ran while one was open for 21% of the time, Pallas kernels for 9%

profile of v3, /device:TPU:0, one launch (start us, length us, event | category | flops | bytes accessed | tf_op | source)
XLA Modules:
  0.0 430.2 jit_solution(10732946351024052007)
XLA Ops:
  13.0 7.6 %collective-permute-done.2 = bf16[144,1536]{1,0:T(8,128)(2,1)S(1)} collective-permute-done((bf16[144,1536]{1,0:T(8,128)(2,1)S(1)}, bf16[144,1536]{1,0:T(8,128)(2,1)S(1)}, u32[]{:S(2)}, u32[]{:S(2)}) %collective-permute-start.2) | collective-permute-done | bytes 442400 | tf_op jit(solution)/shard_map/ppermute | solution.py:26
  20.6 10.5 %collective-permute-done.3 = bf16[144,1536]{1,0:T(8,128)(2,1)S(1)} collective-permute-done((bf16[144,1536]{1,0:T(8,128)(2,1)S(1)}, bf16[144,1536]{1,0:T(8,128)(2,1)S(1)}, u32[]{:S(2)}, u32[]{:S(2)}) %collective-permute-start.3) | collective-permute-done | bytes 442400 | tf_op jit(solution)/shard_map/ppermute | solution.py:26
  54.9 19.3 %collective-permute-done.11 = bf16[6,64,256]{2,1,0:T(8,128)(2,1)S(1)} collective-permute-done((bf16[6,64,256]{2,1,0:T(8,128)(2,1)}, bf16[6,64,256]{2,1,0:T(8,128)(2,1)S(1)}, u32[]{:S(2)}, u32[]{:S(2)}) %collective-permute-start.11) | collective-permute-done | bytes 196640 | tf_op jit(solution)/shard_map/ppermute | solution.py:26
  74.3 8.6 %attend.2 = (bf16[9,64,256]{2,1,0:T(8,128)(2,1)S(1)}, f32[9,1,256]{2,1,0:T(1,128)S(1)}) custom-call(bf16[9,64,256]{2,1,0:T(8,128)(2,1)S(1)} %maximum_multiply_fusion.q_ref, bf16[6,64,1024]{2,1,0:T(8,128)(2,1)S(1)} %pad_maximum_fusion.2.k_ref.v_ref, bf16[6,64,1024]{2,1,0:T(8,128)(2,1)S(1)} %pad_maximum_fusion.2.k_ref.v_ref, s32[1,256]{1,0:T(1,128)S(1)} %bitcast.144, ...), custom_call_target="tpu_custom_call" | custom-call | flops 603979776 | bytes 2097152 | tf_op jit(solution)/shard_map/attend/pallas_call | solution.py:111
  87.6 5.4 %reshape.264 = bf16[1536,576]{1,0:T(8,128)(2,1)} reshape(bf16[576,1536]{1,0:T(8,128)(2,1)} %get-tuple-element.170) | data formatting | bytes 3538944 | tf_op jit(solution)/shard_map/reshape | solution.py:288
  101.2 4.1 multiply_convert_fusion.5
  106.3 10.2 %collective-permute-done.18 = bf16[144,1536]{1,0:T(8,128)(2,1)S(1)} collective-permute-done((bf16[144,1536]{1,0:T(8,128)(2,1)}, bf16[144,1536]{1,0:T(8,128)(2,1)S(1)}, u32[]{:S(2)}, u32[]{:S(2)}) %collective-permute-start.18) | collective-permute-done | bytes 442400 | tf_op jit(solution)/shard_map/ppermute | solution.py:26
  117.9 3.6 collective-permute-done.20
  133.7 21.6 %collective-permute-done.22 = bf16[6,64,256]{2,1,0:T(8,128)(2,1)S(1)} collective-permute-done((bf16[6,64,256]{2,1,0:T(8,128)(2,1)S(1)}, bf16[6,64,256]{2,1,0:T(8,128)(2,1)S(1)}, u32[]{:S(2)}, u32[]{:S(2)}) %collective-permute-start.22) | collective-permute-done | bytes 196640 | tf_op jit(solution)/shard_map/ppermute | solution.py:26
  155.4 8.2 %attend.3 = (bf16[9,64,256]{2,1,0:T(8,128)(2,1)S(1)}, f32[9,1,256]{2,1,0:T(1,128)S(1)}) custom-call(bf16[9,64,256]{2,1,0:T(8,128)(2,1)S(1)} %maximum_multiply_fusion.1.q_ref, bf16[6,64,1024]{2,1,0:T(8,128)(2,1)S(1)} %pad_maximum_fusion.3.k_ref.v_ref, bf16[6,64,1024]{2,1,0:T(8,128)(2,1)S(1)} %pad_maximum_fusion.3.k_ref.v_ref, s32[1,256]{1,0:T(1,128)S(1)} %bitcast.145, ...), custom_call_target="tpu_custom_call" | custom-call | flops 603979776 | bytes 2097152 | tf_op jit(solution)/shard_map/attend/pallas_call | solution.py:111
  168.2 5.4 %reshape.266 = bf16[1536,576]{1,0:T(8,128)(2,1)} reshape(bf16[576,1536]{1,0:T(8,128)(2,1)} %get-tuple-element.168) | data formatting | bytes 3538944 | tf_op jit(solution)/shard_map/reshape | solution.py:288
  179.8 3.1 multiply_convert_fusion.3
  195.3 11.4 %attend_back.2 = (f32[9,64,256]{2,1,0:T(8,128)S(1)}, f32[3,64,1024]{2,1,0:T(8,128)S(1)}, f32[3,64,1024]{2,1,0:T(8,128)S(1)}) custom-call(bf16[9,64,256]{2,1,0:T(8,128)(2,1)S(1)} %copy-done.12, bf16[6,64,1024]{2,1,0:T(8,128)(2,1)S(1)} %pad_maximum_fusion.3.k_ref.v_ref, bf16[6,64,1024]{2,1,0:T(8,128)(2,1)S(1)} %pad_maximum_fusion.3.k_ref.v_ref, ...), custom_call_target="tpu_custom_call" | custom-call | flops 1509949440 | bytes 4194304 | tf_op jit(solution)/shard_map/attend_back/pallas_call | solution.py:133
  207.6 3.9 copy.51
  211.5 5.3 %reshape.269 = bf16[576,1536]{1,0:T(8,128)(2,1)} reshape(bf16[1536,576]{1,0:T(8,128)(2,1)} %copy.51) | data formatting | bytes 3538944 | tf_op jit(solution)/shard_map/reshape | solution.py:355
  232.3 3.8 collective-permute-done.31
  255.6 4.2 reshape.270
  268.9 3.6 collective-permute-start.40
  276.3 11.7 %attend_back.3 = (f32[9,64,256]{2,1,0:T(8,128)S(1)}, f32[3,64,1024]{2,1,0:T(8,128)S(1)}, f32[3,64,1024]{2,1,0:T(8,128)S(1)}) custom-call(bf16[9,64,256]{2,1,0:T(8,128)(2,1)S(1)} %copy-done.10, bf16[6,64,1024]{2,1,0:T(8,128)(2,1)S(1)} %pad_maximum_fusion.2.k_ref.v_ref, bf16[6,64,1024]{2,1,0:T(8,128)(2,1)S(1)} %pad_maximum_fusion.2.k_ref.v_ref, ...), custom_call_target="tpu_custom_call" | custom-call | flops 1509949440 | bytes 4194304 | tf_op jit(solution)/shard_map/attend_back/pallas_call | solution.py:133
  295.4 5.1 %collective-permute-done.48 = bf16[144,384]{1,0:T(8,128)(2,1)S(1)} collective-permute-done((bf16[144,384]{1,0:T(8,128)(2,1)S(1)}, bf16[144,384]{1,0:T(8,128)(2,1)S(1)}, u32[]{:S(2)}, u32[]{:S(2)}) %collective-permute-start.48) | collective-permute-done | bytes 110624 | tf_op jit(solution)/shard_map/ppermute | solution.py:26
  304.2 4.1 collective-permute-done.41
  325.8 6.7 %collective-permute-done.52 = bf16[144,1536]{1,0:T(8,128)(2,1)S(1)} collective-permute-done((bf16[144,1536]{1,0:T(8,128)(2,1)}, bf16[144,1536]{1,0:T(8,128)(2,1)S(1)}, u32[]{:S(2)}, u32[]{:S(2)}) %collective-permute-start.52) | collective-permute-done | bytes 442400 | tf_op jit(solution)/shard_map/ppermute | solution.py:26
  332.5 7.2 %collective-permute-done.51 = bf16[144,1536]{1,0:T(8,128)(2,1)S(1)} collective-permute-done((bf16[144,1536]{1,0:T(8,128)(2,1)S(1)}, bf16[144,1536]{1,0:T(8,128)(2,1)S(1)}, u32[]{:S(2)}, u32[]{:S(2)}) %collective-permute-start.51) | collective-permute-done | bytes 442400 | tf_op jit(solution)/shard_map/ppermute | solution.py:26
  340.1 3.2 collective-permute-done.82
  354.0 4.6 %collective-permute-start.58 = (bf16[144,384]{1,0:T(8,128)(2,1)S(1)}, bf16[144,384]{1,0:T(8,128)(2,1)S(1)}, u32[]{:S(2)}, u32[]{:S(2)}) collective-permute-start(bf16[144,384]{1,0:T(8,128)(2,1)S(1)} %get-tuple-element.214), channel_id=1, source_target_pairs={{0,4},{4,0},{8,12},{12,8},{1,5},{5,1},{9,13},{13,9},{2,6},{6,2},{1... | collective-permute-start | bytes 331784 | tf_op jit(solution)/shard_map/ppermute | solution.py:26
  358.6 4.8 %collective-permute-done.56 = bf16[144,384]{1,0:T(8,128)(2,1)S(1)} collective-permute-done((bf16[144,384]{1,0:T(8,128)(2,1)S(1)}, bf16[144,384]{1,0:T(8,128)(2,1)S(1)}, u32[]{:S(2)}, u32[]{:S(2)}) %collective-permute-start.56) | collective-permute-done | bytes 110624 | tf_op jit(solution)/shard_map/ppermute | solution.py:26
  367.2 10.0 %collective-permute-done.63 = bf16[144,1536]{1,0:T(8,128)(2,1)S(1)} collective-permute-done((bf16[144,1536]{1,0:T(8,128)(2,1)S(1)}, bf16[144,1536]{1,0:T(8,128)(2,1)S(1)}, u32[]{:S(2)}, u32[]{:S(2)}) %collective-permute-start.63) | collective-permute-done | bytes 442400 | tf_op jit(solution)/shard_map/ppermute | solution.py:26
  377.2 4.7 %collective-permute-done.62 = bf16[144,1536]{1,0:T(8,128)(2,1)S(1)} collective-permute-done((bf16[144,1536]{1,0:T(8,128)(2,1)S(1)}, bf16[144,1536]{1,0:T(8,128)(2,1)S(1)}, u32[]{:S(2)}, u32[]{:S(2)}) %collective-permute-start.62) | collective-permute-done | bytes 442400 | tf_op jit(solution)/shard_map/ppermute | solution.py:26
  389.9 3.4 collective-permute-done.66
  395.3 7.9 %collective-permute-done.65 = bf16[144,384]{1,0:T(8,128)(2,1)S(1)} collective-permute-done((bf16[144,384]{1,0:T(8,128)(2,1)S(1)}, bf16[144,384]{1,0:T(8,128)(2,1)S(1)}, u32[]{:S(2)}, u32[]{:S(2)}) %collective-permute-start.65) | collective-permute-done | bytes 110624 | tf_op jit(solution)/shard_map/ppermute | solution.py:26
  412.6 3.1 collective-permute-done.76
  418.1 5.9 %collective-permute-done.68 = bf16[144,384]{1,0:T(8,128)(2,1)S(1)} collective-permute-done((bf16[144,384]{1,0:T(8,128)(2,1)S(1)}, bf16[144,384]{1,0:T(8,128)(2,1)S(1)}, u32[]{:S(2)}, u32[]{:S(2)}) %collective-permute-start.68) | collective-permute-done | bytes 110624 | tf_op jit(solution)/shard_map/ppermute | solution.py:26
  (489 shorter events, 205.0 us)
Async XLA Ops:
  4.5 28.0 %collective-permute-start.6 = (bf16[2,144]{1,0:T(2,128)(2,1)S(1)}, bf16[2,144]{1,0:T(2,128)(2,1)S(1)}, u32[]{:S(2)}, u32[]{:S(2)}) collective-permute-start(bf16[2,144]{1,0:T(2,128)(2,1)S(1)} %pad_maximum_fusion.13), channel_id=1, source_target_pairs={{0,16},{16,0},{1,17},{17,1},{2,18},{18,2},{3,19},{19,3},{4,20},{20... | collective-permute-start | bytes 1736 | tf_op jit(solution)/shard_map/ppermute | solution.py:26
  9.7 21.4 %collective-permute-start.3 = (bf16[144,1536]{1,0:T(8,128)(2,1)S(1)}, bf16[144,1536]{1,0:T(8,128)(2,1)S(1)}, u32[]{:S(2)}, u32[]{:S(2)}) collective-permute-start(bf16[144,1536]{1,0:T(8,128)(2,1)S(1)} %get-tuple-element.66), channel_id=1, source_target_pairs={{0,2},{1,3},{2,0},{3,1},{4,6},{5,7},{6,4},{7,5},{8,10},{9,11},{10,... | collective-permute-start | bytes 1327112 | tf_op jit(solution)/shard_map/ppermute | solution.py:26
  11.2 19.9 %collective-permute-start.4 = (bf16[144,1536]{1,0:T(8,128)(2,1)S(1)}, bf16[144,1536]{1,0:T(8,128)(2,1)S(1)}, u32[]{:S(2)}, u32[]{:S(2)}) collective-permute-start(bf16[144,1536]{1,0:T(8,128)(2,1)S(1)} %get-tuple-element.66), channel_id=1, source_target_pairs={{0,3},{1,2},{2,1},{3,0},{4,7},{5,6},{6,5},{7,4},{8,11},{9,10},{10,... | collective-permute-start | bytes 1327112 | tf_op jit(solution)/shard_map/ppermute | solution.py:26
  46.0 36.9 %collective-permute-start.13 = (bf16[144,1536]{1,0:T(8,128)(2,1)S(1)}, bf16[144,1536]{1,0:T(8,128)(2,1)S(1)}, u32[]{:S(2)}, u32[]{:S(2)}) collective-permute-start(bf16[144,1536]{1,0:T(8,128)(2,1)S(1)} %get-tuple-element.74), channel_id=1, source_target_pairs={{0,1},{1,0},{2,3},{3,2},{4,5},{5,4},{6,7},{7,6},{8,9},{9,8},{10,11... | collective-permute-start | bytes 1327112 | tf_op jit(solution)/shard_map/ppermute | solution.py:26
  47.3 35.6 %collective-permute-start.14 = (bf16[144,1536]{1,0:T(8,128)(2,1)S(1)}, bf16[144,1536]{1,0:T(8,128)(2,1)S(1)}, u32[]{:S(2)}, u32[]{:S(2)}) collective-permute-start(bf16[144,1536]{1,0:T(8,128)(2,1)S(1)} %get-tuple-element.74), channel_id=1, source_target_pairs={{0,2},{1,3},{2,0},{3,1},{4,6},{5,7},{6,4},{7,5},{8,10},{9,11},{10,... | collective-permute-start | bytes 1327112 | tf_op jit(solution)/shard_map/ppermute | solution.py:26
  48.2 34.8 %collective-permute-start.15 = (bf16[144,1536]{1,0:T(8,128)(2,1)S(1)}, bf16[144,1536]{1,0:T(8,128)(2,1)S(1)}, u32[]{:S(2)}, u32[]{:S(2)}) collective-permute-start(bf16[144,1536]{1,0:T(8,128)(2,1)S(1)} %get-tuple-element.74), channel_id=1, source_target_pairs={{0,3},{1,2},{2,1},{3,0},{4,7},{5,6},{6,5},{7,4},{8,11},{9,10},{10,... | collective-permute-start | bytes 1327112 | tf_op jit(solution)/shard_map/ppermute | solution.py:26
  49.6 24.6 %collective-permute-start.11 = (bf16[6,64,256]{2,1,0:T(8,128)(2,1)}, bf16[6,64,256]{2,1,0:T(8,128)(2,1)S(1)}, u32[]{:S(2)}, u32[]{:S(2)}) collective-permute-start(bf16[6,64,256]{2,1,0:T(8,128)(2,1)} %pad_maximum_fusion.9), channel_id=1, source_target_pairs={{0,2},{1,3},{2,0},{3,1},{4,6},{5,7},{6,4},{7,5},{8,10},{9,11},{10,... | collective-permute-start | bytes 589832 | tf_op jit(solution)/shard_map/ppermute | solution.py:26
  53.3 20.9 %collective-permute-start.10 = (bf16[6,64,256]{2,1,0:T(8,128)(2,1)}, bf16[6,64,256]{2,1,0:T(8,128)(2,1)S(1)}, u32[]{:S(2)}, u32[]{:S(2)}) collective-permute-start(bf16[6,64,256]{2,1,0:T(8,128)(2,1)} %pad_maximum_fusion.9), channel_id=1, source_target_pairs={{0,1},{1,0},{2,3},{3,2},{4,5},{5,4},{6,7},{7,6},{8,9},{9,8},{10,11... | collective-permute-start | bytes 589832 | tf_op jit(solution)/shard_map/ppermute | solution.py:26
  94.4 22.0 %collective-permute-start.18 = (bf16[144,1536]{1,0:T(8,128)(2,1)}, bf16[144,1536]{1,0:T(8,128)(2,1)S(1)}, u32[]{:S(2)}, u32[]{:S(2)}) collective-permute-start(bf16[144,1536]{1,0:T(8,128)(2,1)} %get-tuple-element.80), channel_id=1, source_target_pairs={{0,2},{1,3},{2,0},{3,1},{4,6},{5,7},{6,4},{7,5},{8,10},{9,11},{10,... | collective-permute-start | bytes 1327112 | tf_op jit(solution)/shard_map/ppermute | solution.py:26
  95.0 21.4 %collective-permute-start.19 = (bf16[144,1536]{1,0:T(8,128)(2,1)}, bf16[144,1536]{1,0:T(8,128)(2,1)S(1)}, u32[]{:S(2)}, u32[]{:S(2)}) collective-permute-start(bf16[144,1536]{1,0:T(8,128)(2,1)} %get-tuple-element.80), channel_id=1, source_target_pairs={{0,3},{1,2},{2,1},{3,0},{4,7},{5,6},{6,5},{7,4},{8,11},{9,10},{10,... | collective-permute-start | bytes 1327112 | tf_op jit(solution)/shard_map/ppermute | solution.py:26
  125.5 38.1 %collective-permute-start.24 = (bf16[144,1536]{1,0:T(8,128)(2,1)S(1)}, bf16[144,1536]{1,0:T(8,128)(2,1)S(1)}, u32[]{:S(2)}, u32[]{:S(2)}) collective-permute-start(bf16[144,1536]{1,0:T(8,128)(2,1)S(1)} %copy-done.49), channel_id=1, source_target_pairs={{0,1},{1,0},{2,3},{3,2},{4,5},{5,4},{6,7},{7,6},{8,9},{9,8},{10,11... | collective-permute-start | bytes 1327112 | tf_op jit(solution)/shard_map/ppermute | solution.py:26
  126.4 37.3 %collective-permute-start.25 = (bf16[144,1536]{1,0:T(8,128)(2,1)S(1)}, bf16[144,1536]{1,0:T(8,128)(2,1)S(1)}, u32[]{:S(2)}, u32[]{:S(2)}) collective-permute-start(bf16[144,1536]{1,0:T(8,128)(2,1)S(1)} %copy-done.49), channel_id=1, source_target_pairs={{0,2},{1,3},{2,0},{3,1},{4,6},{5,7},{6,4},{7,5},{8,10},{9,11},{10,... | collective-permute-start | bytes 1327112 | tf_op jit(solution)/shard_map/ppermute | solution.py:26
  127.8 35.8 %collective-permute-start.26 = (bf16[144,1536]{1,0:T(8,128)(2,1)S(1)}, bf16[144,1536]{1,0:T(8,128)(2,1)S(1)}, u32[]{:S(2)}, u32[]{:S(2)}) collective-permute-start(bf16[144,1536]{1,0:T(8,128)(2,1)S(1)} %copy-done.49), channel_id=1, source_target_pairs={{0,3},{1,2},{2,1},{3,0},{4,7},{5,6},{6,5},{7,4},{8,11},{9,10},{10,... | collective-permute-start | bytes 1327112 | tf_op jit(solution)/shard_map/ppermute | solution.py:26
  129.0 26.3 %collective-permute-start.22 = (bf16[6,64,256]{2,1,0:T(8,128)(2,1)S(1)}, bf16[6,64,256]{2,1,0:T(8,128)(2,1)S(1)}, u32[]{:S(2)}, u32[]{:S(2)}) collective-permute-start(bf16[6,64,256]{2,1,0:T(8,128)(2,1)S(1)} %pad_maximum_fusion.10), channel_id=1, source_target_pairs={{0,2},{1,3},{2,0},{3,1},{4,6},{5,7},{6,4},{7,5},{8,10},{9,11},{10,... | collective-permute-start | bytes 589832 | tf_op jit(solution)/shard_map/ppermute | solution.py:26
  133.0 22.3 %collective-permute-start.21 = (bf16[6,64,256]{2,1,0:T(8,128)(2,1)S(1)}, bf16[6,64,256]{2,1,0:T(8,128)(2,1)S(1)}, u32[]{:S(2)}, u32[]{:S(2)}) collective-permute-start(bf16[6,64,256]{2,1,0:T(8,128)(2,1)S(1)} %pad_maximum_fusion.10), channel_id=1, source_target_pairs={{0,1},{1,0},{2,3},{3,2},{4,5},{5,4},{6,7},{7,6},{8,9},{9,8},{10,11... | collective-permute-start | bytes 589832 | tf_op jit(solution)/shard_map/ppermute | solution.py:26
  184.6 33.9 %collective-permute-start.28 = (bf16[256,576]{0,1:T(8,128)(2,1)}, bf16[256,576]{0,1:T(8,128)(2,1)}, u32[]{:S(2)}, u32[]{:S(2)}) collective-permute-start(bf16[256,576]{0,1:T(8,128)(2,1)} %get-tuple-element.251), channel_id=1, source_target_pairs={{0,16},{16,0},{1,17},{17,1},{2,18},{18,2},{3,19},{19,3},{4,20},{20... | collective-permute-start | bytes 884744 | tf_op jit(solution)/shard_map/ppermute | solution.py:26
  188.3 32.4 %collective-permute-start.29 = (bf16[576,1536]{1,0:T(8,128)(2,1)}, bf16[576,1536]{1,0:T(8,128)(2,1)}, u32[]{:S(2)}, u32[]{:S(2)}) collective-permute-start(bf16[576,1536]{1,0:T(8,128)(2,1)} %get-tuple-element.254), channel_id=1, source_target_pairs={{0,16},{16,0},{1,17},{17,1},{2,18},{18,2},{3,19},{19,3},{4,20},{20... | collective-permute-start | bytes 5308424 | tf_op jit(solution)/shard_map/ppermute | solution.py:26
  227.7 34.2 %collective-permute-start.35 = (bf16[144,1536]{1,0:T(8,128)(2,1)}, bf16[144,1536]{1,0:T(8,128)(2,1)}, u32[]{:S(2)}, u32[]{:S(2)}) collective-permute-start(bf16[144,1536]{1,0:T(8,128)(2,1)} %get-tuple-element.187), channel_id=1, source_target_pairs={{0,3},{1,2},{2,1},{3,0},{4,7},{5,6},{6,5},{7,4},{8,11},{9,10},{10,... | collective-permute-start | bytes 1327112 | tf_op jit(solution)/shard_map/ppermute | solution.py:26
  228.9 33.0 %collective-permute-start.34 = (bf16[144,1536]{1,0:T(8,128)(2,1)}, bf16[144,1536]{1,0:T(8,128)(2,1)}, u32[]{:S(2)}, u32[]{:S(2)}) collective-permute-start(bf16[144,1536]{1,0:T(8,128)(2,1)} %get-tuple-element.188), channel_id=1, source_target_pairs={{0,2},{1,3},{2,0},{3,1},{4,6},{5,7},{6,4},{7,5},{8,10},{9,11},{10,... | collective-permute-start | bytes 1327112 | tf_op jit(solution)/shard_map/ppermute | solution.py:26
  231.8 30.1 %collective-permute-start.33 = (bf16[144,1536]{1,0:T(8,128)(2,1)}, bf16[144,1536]{1,0:T(8,128)(2,1)}, u32[]{:S(2)}, u32[]{:S(2)}) collective-permute-start(bf16[144,1536]{1,0:T(8,128)(2,1)} %get-tuple-element.186), channel_id=1, source_target_pairs={{0,1},{1,0},{2,3},{3,2},{4,5},{5,4},{6,7},{7,6},{8,9},{9,8},{10,11... | collective-permute-start | bytes 1327112 | tf_op jit(solution)/shard_map/ppermute | solution.py:26
  242.0 21.8 %collective-permute-start.36 = (bf16[576,1536]{1,0:T(8,128)(2,1)}, bf16[576,1536]{1,0:T(8,128)(2,1)}, u32[]{:S(2)}, u32[]{:S(2)}) collective-permute-start(bf16[576,1536]{1,0:T(8,128)(2,1)} %broadcast_select_fusion.2), channel_id=1, source_target_pairs={{0,16},{16,0},{1,17},{17,1},{2,18},{18,2},{3,19},{19,3},{4,20},{20... | collective-permute-start | bytes 5308424 | tf_op jit(solution)/shard_map/ppermute | solution.py:26
  247.9 18.8 %collective-permute-start.37 = (bf16[576,1536]{1,0:T(8,128)(2,1)}, bf16[576,1536]{1,0:T(8,128)(2,1)}, u32[]{:S(2)}, u32[]{:S(2)}) collective-permute-start(bf16[576,1536]{1,0:T(8,128)(2,1)} %get-tuple-element.258), channel_id=1, source_target_pairs={{0,16},{16,0},{1,17},{17,1},{2,18},{18,2},{3,19},{19,3},{4,20},{20... | collective-permute-start | bytes 5308424 | tf_op jit(solution)/shard_map/ppermute | solution.py:26
  268.9 19.1 %collective-permute-start.40 = (bf16[144,384]{1,0:T(8,128)(2,1)S(1)}, bf16[144,384]{1,0:T(8,128)(2,1)S(1)}, u32[]{:S(2)}, u32[]{:S(2)}) collective-permute-start(bf16[144,384]{1,0:T(8,128)(2,1)S(1)} %get-tuple-element.221), channel_id=1, source_target_pairs={{0,12},{4,8},{8,4},{12,0},{1,13},{5,9},{9,5},{13,1},{2,14},{6,10},... | collective-permute-start | bytes 331784 | tf_op jit(solution)/shard_map/ppermute | solution.py:26
  274.4 47.2 %collective-permute-start.46 = (bf16[144,1536]{1,0:T(8,128)(2,1)S(1)}, bf16[144,1536]{1,0:T(8,128)(2,1)S(1)}, u32[]{:S(2)}, u32[]{:S(2)}) collective-permute-start(bf16[144,1536]{1,0:T(8,128)(2,1)S(1)} %get-tuple-element.184), channel_id=1, source_target_pairs={{0,3},{1,2},{2,1},{3,0},{4,7},{5,6},{6,5},{7,4},{8,11},{9,10},{10,... | collective-permute-start | bytes 1327112 | tf_op jit(solution)/shard_map/ppermute | solution.py:26
  301.5 21.4 %collective-permute-start.45 = (bf16[144,1536]{1,0:T(8,128)(2,1)}, bf16[144,1536]{1,0:T(8,128)(2,1)S(1)}, u32[]{:S(2)}, u32[]{:S(2)}) collective-permute-start(bf16[144,1536]{1,0:T(8,128)(2,1)} %get-tuple-element.185), channel_id=1, source_target_pairs={{0,2},{1,3},{2,0},{3,1},{4,6},{5,7},{6,4},{7,5},{8,10},{9,11},{10,... | collective-permute-start | bytes 1327112 | tf_op jit(solution)/shard_map/ppermute | solution.py:26
  303.0 19.9 %collective-permute-start.44 = (bf16[144,1536]{1,0:T(8,128)(2,1)}, bf16[144,1536]{1,0:T(8,128)(2,1)S(1)}, u32[]{:S(2)}, u32[]{:S(2)}) collective-permute-start(bf16[144,1536]{1,0:T(8,128)(2,1)} %get-tuple-element.183), channel_id=1, source_target_pairs={{0,1},{1,0},{2,3},{3,2},{4,5},{5,4},{6,7},{7,6},{8,9},{9,8},{10,11... | collective-permute-start | bytes 1327112 | tf_op jit(solution)/shard_map/ppermute | solution.py:26
  320.6 19.0 %collective-permute-start.51 = (bf16[144,1536]{1,0:T(8,128)(2,1)S(1)}, bf16[144,1536]{1,0:T(8,128)(2,1)S(1)}, u32[]{:S(2)}, u32[]{:S(2)}) collective-permute-start(bf16[144,1536]{1,0:T(8,128)(2,1)S(1)} %get-tuple-element.182), channel_id=1, source_target_pairs={{0,2},{1,3},{2,0},{3,1},{4,6},{5,7},{6,4},{7,5},{8,10},{9,11},{10,... | collective-permute-start | bytes 1327112 | tf_op jit(solution)/shard_map/ppermute | solution.py:26
  321.6 18.1 %collective-permute-start.50 = (bf16[144,1536]{1,0:T(8,128)(2,1)S(1)}, bf16[144,1536]{1,0:T(8,128)(2,1)S(1)}, u32[]{:S(2)}, u32[]{:S(2)}) collective-permute-start(bf16[144,1536]{1,0:T(8,128)(2,1)S(1)} %get-tuple-element.180), channel_id=1, source_target_pairs={{0,1},{1,0},{2,3},{3,2},{4,5},{5,4},{6,7},{7,6},{8,9},{9,8},{10,11... | collective-permute-start | bytes 1327112 | tf_op jit(solution)/shard_map/ppermute | solution.py:26
  322.9 22.1 %collective-permute-start.54 = (bf16[576,1536]{1,0:T(8,128)(2,1)S(1)}, bf16[576,1536]{1,0:T(8,128)(2,1)S(1)}, u32[]{:S(2)}, u32[]{:S(2)}) collective-permute-start(bf16[576,1536]{1,0:T(8,128)(2,1)S(1)} %broadcast_select_fusion), channel_id=1, source_target_pairs={{0,16},{16,0},{1,17},{17,1},{2,18},{18,2},{3,19},{19,3},{4,20},{20... | collective-permute-start | bytes 5308424 | tf_op jit(solution)/shard_map/ppermute | solution.py:26
  382.1 33.7 %collective-permute-start.70 = (bf16[144,384]{1,0:T(8,128)(2,1)S(1)}, bf16[144,384]{1,0:T(8,128)(2,1)S(1)}, u32[]{:S(2)}, u32[]{:S(2)}) collective-permute-start(bf16[144,384]{1,0:T(8,128)(2,1)S(1)} %add_convert_fusion.13), channel_id=1, source_target_pairs={{0,4},{4,0},{8,12},{12,8},{1,5},{5,1},{9,13},{13,9},{2,6},{6,2},{1... | collective-permute-start | bytes 331784 | tf_op jit(solution)/shard_map/ppermute | solution.py:26
  382.2 35.5 %collective-permute-start.71 = (bf16[144,384]{1,0:T(8,128)(2,1)S(1)}, bf16[144,384]{1,0:T(8,128)(2,1)S(1)}, u32[]{:S(2)}, u32[]{:S(2)}) collective-permute-start(bf16[144,384]{1,0:T(8,128)(2,1)S(1)} %add_convert_fusion.13), channel_id=1, source_target_pairs={{0,8},{4,12},{8,0},{12,4},{1,9},{5,13},{9,1},{13,5},{2,10},{6,14},... | collective-permute-start | bytes 331784 | tf_op jit(solution)/shard_map/ppermute | solution.py:26
  393.3 24.5 %collective-permute-start.72 = (bf16[144,384]{1,0:T(8,128)(2,1)S(1)}, bf16[144,384]{1,0:T(8,128)(2,1)S(1)}, u32[]{:S(2)}, u32[]{:S(2)}) collective-permute-start(bf16[144,384]{1,0:T(8,128)(2,1)S(1)} %add_convert_fusion.13), channel_id=1, source_target_pairs={{0,12},{4,8},{8,4},{12,0},{1,13},{5,9},{9,5},{13,1},{2,14},{6,10},... | collective-permute-start | bytes 331784 | tf_op jit(solution)/shard_map/ppermute | solution.py:26
  (125 other events, 989.2 us)
